TPU v7x, 256 devices: a whole 4x4x8 slice. The times are simulated.
256 devices in a mesh: sub: 128 (over x, z, y), section: 2 (over core).
Axes of the slice: x: 4, y: 4, z: 8, core: 2. Of those that a mesh axis runs over, the one named last changes fastest.
Arguments:
- voltages: bfloat16 [256, 2, 48, 16384], P('sub', None, None, 'section'), may hold values from -6 to 6
- delay_table: float32 [64], replicated, may hold values from -4 to 4
- delay_index: int32 [128, 48], replicated, may hold values from 0 to 63
- dm_table: float32 [32], replicated, may hold values from 0.05 to 0.4
- dm_index: int32 [128], replicated, may hold values from 0 to 31
- range_bounds: int32 [128, 2], replicated, may hold values from 0 to 256, as said below
Outputs:
- dedispersed: bfloat16 [128, 256, 2, 16384], P('sub', None, None, 'section')
Inputs may be any that keep to these rules, and one draw needn't show every extreme that they name: `range_bounds`: each beam's range has 64 to 128 subbands and lies within the 256 subbands; some beam has exactly 128.
All inputs are finite; a program needn't handle non-finite values.
Results may differ from a plain program's by a relative error of at most 0.0059.
Values may be sent and summed in bfloat16 or wider, within the bound.
A program may use at most 128 MiB of HBM per device.

v0:
```python
import math

import jax
import jax.numpy as jnp
from jax import lax
from jax.sharding import PartitionSpec as P

PRECISE = lax.Precision.HIGH


def partner_2(value, axis, bit):
    mask = 2**bit
    pairs = [(source, source ^ mask) for source in range(lax.axis_size(axis))]
    return lax.ppermute(value, axis, pairs)


def beam_weights(delays, frequency, stations):
    angles = (2.0 * math.pi * delays)[..., None, :] * frequency[:, None]
    scaling = 1.0 / math.sqrt(stations)
    return (
        (jnp.cos(angles) * scaling).astype(jnp.bfloat16),
        (-jnp.sin(angles) * scaling).astype(jnp.bfloat16),
    )


def signed_bins(bin_index, length):
    return jnp.where(bin_index < length // 2, bin_index, bin_index - length).astype(jnp.float32)


def chirp_phase(dispersion, frequency, bin_values, length):
    coefficient = math.pi * dispersion / (length * (frequency * frequency * frequency))
    return coefficient.reshape(coefficient.shape + (1,) * bin_values.ndim) * (
        bin_values * bin_values
    )


def factor_sizes(length):
    inner_size = min(128, length)
    return (length // inner_size, inner_size)


def twiddle_angle(left_index, right_index, length, direction):
    product = left_index[:, None] * right_index[None, :] % length
    return direction * 2.0 * math.pi * product.astype(jnp.float32) / length


def complex_table(angles):
    cosine = jnp.cos(angles)
    sine = jnp.sin(angles)
    from_real = jnp.stack([cosine, sine], axis=1)
    from_imag = jnp.stack([-sine, cosine], axis=1)
    return jnp.stack([from_real, from_imag], axis=0)


def rotate(values, angles):
    cosine = jnp.cos(angles)
    sine = jnp.sin(angles)
    real_part = values[:, 0]
    imag_part = values[:, 1]
    return jnp.stack(
        [real_part * cosine - imag_part * sine, real_part * sine + imag_part * cosine], axis=1
    )


def forward_dft(series):
    row_count = series.shape[0]
    length = series.shape[2]
    outer_size, inner_size = factor_sizes(length)
    grid_view = series.reshape(row_count, 2, outer_size, inner_size)
    outer_index = jnp.arange(outer_size)
    inner_index = jnp.arange(inner_size)
    first_table = complex_table(twiddle_angle(outer_index, outer_index, outer_size, -1.0))
    partial_sums = jnp.einsum("rcpq,cpdk->rdkq", grid_view, first_table, precision=PRECISE)
    partial_sums = rotate(partial_sums, twiddle_angle(outer_index, inner_index, length, -1.0))
    second_table = complex_table(twiddle_angle(inner_index, inner_index, inner_size, -1.0))
    return jnp.einsum("rckq,cqdj->rdkj", partial_sums, second_table, precision=PRECISE)


def inverse_dft(spectrum):
    row_count = spectrum.shape[0]
    outer_size = spectrum.shape[2]
    inner_size = spectrum.shape[3]
    length = outer_size * inner_size
    outer_index = jnp.arange(outer_size)
    inner_index = jnp.arange(inner_size)
    inner_table = complex_table(twiddle_angle(inner_index, inner_index, inner_size, 1.0))
    partial_sums = jnp.einsum("rckj,cjdq->rdkq", spectrum, inner_table, precision=PRECISE)
    partial_sums = rotate(partial_sums, twiddle_angle(outer_index, inner_index, length, 1.0))
    outer_table = complex_table(twiddle_angle(outer_index, outer_index, outer_size, 1.0))
    result_grid = jnp.einsum("rckq,ckdp->rdpq", partial_sums, outer_table, precision=PRECISE)
    return result_grid.reshape(row_count, 2, length)


def bin_order(length):
    outer_size, inner_size = factor_sizes(length)
    return jnp.arange(outer_size)[:, None] + outer_size * jnp.arange(inner_size)[None, :]


def row_frequency(row_ids, subbands):
    return 1.0 + (row_ids.astype(jnp.float32) + 0.5) / subbands


def per_device(voltages, delay_table, delay_index, dm_table, dm_index, range_bounds):
    local_subbands = voltages.shape[0]
    stations = voltages.shape[2]
    half_length = voltages.shape[3]
    subbands = local_subbands * lax.axis_size("sub")
    window_rows = subbands // 2 + 2
    full_length = half_length * lax.axis_size("section")
    sub_index = lax.axis_index("sub")
    section_index = lax.axis_index("section")
    local_ids = sub_index * local_subbands + jnp.arange(local_subbands)
    local_freq = row_frequency(local_ids, subbands)
    picked = delay_index[:, :, None] == jnp.arange(delay_table.shape[0])[None, None, :]
    delays = jnp.sum(jnp.where(picked, delay_table, 0.0), axis=-1)
    w_real, w_imag = beam_weights(delays, local_freq, stations)
    stacked = jnp.stack(
        [jnp.stack([w_real, -w_imag], axis=2), jnp.stack([w_imag, w_real], axis=2)], axis=2
    )
    formed = jnp.einsum("bfocs,fcst->bfot", stacked, voltages, preferred_element_type=jnp.float32)
    starts = range_bounds[:, 0]
    ends = range_bounds[:, 1]
    live_rows = (local_ids[None, :] >= starts[:, None]) & (local_ids[None, :] < ends[:, None])
    beams_local = jnp.where(live_rows[:, :, None, None], formed, 0.0).astype(jnp.bfloat16)
    own_start = lax.dynamic_index_in_dim(starts, sub_index, keepdims=False)
    window_start = jnp.minimum(own_start - own_start % 2, subbands - window_rows)
    own_entry = lax.dynamic_index_in_dim(dm_index, sub_index, keepdims=False)
    dispersion = jnp.sum(jnp.where(jnp.arange(dm_table.shape[0]) == own_entry, dm_table, 0.0))
    turned = lax.all_to_all(beams_local, "sub", split_axis=0, concat_axis=1, tiled=True)[0]
    window = lax.dynamic_slice_in_dim(turned, window_start, window_rows, 0)
    partner = partner_2(window, "section", 0)
    lower_half = jnp.where(section_index == 0, window, partner).astype(jnp.float32)
    upper_half = jnp.where(section_index == 0, partner, window).astype(jnp.float32)
    parity_sign = (1 - 2 * section_index).astype(jnp.float32)
    sample_ids = jnp.arange(half_length)
    merged = lower_half + parity_sign * upper_half
    shift_angle = (
        -2.0
        * math.pi
        * (section_index * sample_ids % full_length).astype(jnp.float32)
        / full_length
    )
    spectrum = forward_dft(rotate(merged, shift_angle))
    bin_values = signed_bins(2 * bin_order(half_length) + section_index, full_length)
    window_freq = row_frequency(window_start + jnp.arange(window_rows), subbands)
    filtered = rotate(spectrum, chirp_phase(dispersion, window_freq, bin_values, full_length))
    partial_result = inverse_dft(filtered)
    remote = partner_2(partial_result, "section", 0)
    even_part = jnp.where(section_index == 0, partial_result, remote)
    odd_part = jnp.where(section_index == 0, remote, partial_result)
    back_angle = 2.0 * math.pi * sample_ids.astype(jnp.float32) / full_length
    odd_part = rotate(odd_part, back_angle)
    result_window = ((even_part + parity_sign * odd_part) * (1.0 / full_length)).astype(
        jnp.bfloat16
    )
    blank = jnp.zeros((subbands, 2, half_length), jnp.bfloat16)
    placed = lax.dynamic_update_slice_in_dim(blank, result_window, window_start, 0)
    return placed[None]


def solution(mesh):
    return jax.shard_map(
        per_device,
        mesh=mesh,
        in_specs=(P("sub", None, None, "section"), P(), P(), P(), P(), P()),
        out_specs=P("sub", None, None, "section"),
        check_vma=False,
    )
```

profile of v0, /device:TPU:1, one launch (start us, length us, event | category | flops | bytes accessed | tf_op | source)
XLA Modules:
  0.0 418.1 jit_solution(4203671722807182825)
XLA Ops:
  0.0 1.3 select_reduce_fusion
  1.9 0.8 slice_bitcast_fusion.1
  2.7 2.4 fusion
  5.1 14.7 %copy.48 = bf16[128,2,2,8192]{3,2,1,0:T(2,128)(2,1)} copy(bf16[128,2,2,8192]{3,0,2,1:T(8,128)(2,1)S(1)} %fusion) | data formatting | bytes 16777216 | tf_op jit(solution)/shard_map/convert_element_type | solution.py:124
  19.8 16.9 %all-to-all-start = ((bf16[128,2,2,8192]{3,2,1,0:T(2,128)(2,1)}), bf16[128,2,2,8192]{3,2,1,0:T(2,128)(2,1)}, u32[]{:S(2)}, u32[]{:S(2)}) async-start(bf16[128,2,2,8192]{3,2,1,0:T(2,128)(2,1)} %copy.48), calls=%async_computation | async-start | bytes 16777216 | tf_op jit(solution)/shard_map/all_to_all | solution.py:129
  36.7 0.6 constant_dynamic-slice_fusion.1
  39.9 179.0 %all-to-all-done = bf16[128,2,2,8192]{3,2,1,0:T(2,128)(2,1)} async-done(((bf16[128,2,2,8192]{3,2,1,0:T(2,128)(2,1)}), bf16[128,2,2,8192]{3,2,1,0:T(2,128)(2,1)}, u32[]{:S(2)}, u32[]{:S(2)}) %all-to-all-start) | async-done | bytes 8388640 | tf_op jit(solution)/shard_map/all_to_all | solution.py:129
  218.9 11.8 %constant_dynamic-slice_fusion = bf16[130,2,8192]{2,1,0:T(2,128)(2,1)} fusion(bf16[256,2,8192]{2,1,0:T(2,128)(2,1)} %bitcast.26, s32[]{:T(128)S(6)} %select_n.211), kind=kLoop, calls=%fused_computation.143 | loop fusion | bytes 8519684 | tf_op jit(solution)/shard_map/dynamic_slice | solution.py:130
  230.6 6.5 %collective-permute-start = (bf16[130,2,8192]{2,1,0:T(2,128)(2,1)}, bf16[130,2,8192]{2,1,0:T(2,128)(2,1)}, u32[]{:S(2)}, u32[]{:S(2)}) collective-permute-start(bf16[130,2,8192]{2,1,0:T(2,128)(2,1)} %constant_dynamic-slice_fusion), channel_id=1, source_target_pairs={{0,1},{1,0},{2,3},{3,2},{4,5},{5,4},{6,7},{7,6},{8,9},{9,8},{10,11... | collective-permute-start | bytes 12779528 | tf_op jit(solution)/shard_map/ppermute | solution.py:14
  237.2 0.6 dynamic_slice.12
  237.8 1.2 fusion.80
  241.3 0.3 multiply_sine_fusion.2
  242.0 2.4 collective-permute-done
  244.4 11.6 %multiply_add_fusion = f32[130,2,8192]{2,1,0:T(2,128)S(1)} fusion(bf16[130,2,8192]{2,1,0:T(2,128)(2,1)} %collective-permute-done, pred[]{:T(512)S(6)} %eq.38, f32[]{:T(128)S(6)} %convert_element_type.214, bf16[256,2,8192]{2,1,0:T(2,128)(2,1)} %bitcast.26, s32[]{:T(128)S(6)} %select_n.211), kind=kLoop, calls=%fused_computation.21 | loop fusion | flops 12779520 | bytes 17039368 | tf_op jit(solution)/shard_map/add | solution.py:136
  256.0 10.6 %multiply_subtract_fusion.3 = (f32[130,1,8192]{2,1,0:T(1,128)S(1)}, f32[130,1,8192]{2,1,0:T(1,128)S(1)}) fusion(f32[130,2,8192]{2,1,0:T(2,128)S(1)} %multiply_add_fusion, f32[8192]{0:T(1024)S(1)} %get-tuple-element.30, f32[8192]{0:T(1024)S(1)} %get-tuple-element.31), kind=kLoop, calls=%fused_computation.42 | loop fusion | flops 6389760 | bytes 17104896 | tf_op jit(solution)/shard_map/sub | solution.py:61
  266.6 4.4 %fusion.31 = f32[130,2,64,128]{3,2,0,1:T(8,128)S(1)} fusion(f32[130,1,64,128]{3,2,1,0:T(8,128)S(1)} %bitcast.112, f32[130,1,64,128]{3,2,1,0:T(8,128)S(1)} %bitcast.111, f32[1,64,2,64]{1,3,0,2:T(8,128)S(1)} %get-tuple-element.24, f32[1,64,2,64]{1,3,0,2:T(8,128)S(1)} %get-tuple-element.23), kind=kOutput, calls=%fused_computation.46 | convolution fusion | flops 1637924864 | bytes 17104896 | tf_op jit(solution)/shard_map/rcpq,cpdk->rdkq/dot_general | solution.py:73
  271.0 2.1 multiply_subtract_fusion.2
  273.1 0.9 pad_maximum_fusion.2
  274.0 16.6 %fusion.22 = f32[130,2,64,128]{3,0,2,1:T(8,128)S(1)} fusion(f32[130,2,64,128]{3,2,0,1:T(8,128)S(1)} %pad_maximum_fusion.2, f32[1,128,2,128]{3,1,0,2:T(8,128)S(1)} %get-tuple-element.20, f32[1,128,2,128]{3,1,0,2:T(8,128)S(1)} %get-tuple-element.19), kind=kOutput, calls=%fused_computation.43 | convolution fusion | flops 3271622656 | bytes 17301504 | tf_op jit(solution)/shard_map/rckq,cqdj->rdkj/dot_general | solution.py:76
  290.6 16.6 %fusion.20 = (f32[130,1,64,128]{3,0,2,1:T(8,128)S(1)}, f32[130,1,64,128]{3,0,2,1:T(8,128)S(1)}) fusion(f32[130,2,64,128]{3,0,2,1:T(8,128)S(1)} %fusion.22, f32[64,128]{1,0:T(8,128)S(1)} %fusion.60, f32[130]{0:T(256)S(1)} %fusion.79), kind=kLoop, calls=%fused_computation.32 | loop fusion | flops 7454720 | bytes 17072648 | tf_op jit(solution)/shard_map/sub | solution.py:61
  307.2 3.8 fusion.25
  311.0 1.1 multiply_subtract_fusion
  312.2 0.6 pad_maximum_fusion.1
  312.8 7.1 %fusion.28 = f32[130,2,64,128]{3,2,0,1:T(8,128)} fusion(f32[130,2,64,128]{3,0,2,1:T(8,128)S(1)} %pad_maximum_fusion.1, f32[1,64,2,64]{1,3,2,0:T(8,128)S(1)} %get-tuple-element.22, f32[1,64,2,64]{1,3,2,0:T(8,128)S(1)} %get-tuple-element.21), kind=kOutput, calls=%fused_computation.45 | convolution fusion | flops 1635794944 | bytes 17104896 | tf_op jit(solution)/shard_map/rckq,ckdp->rdpq/dot_general | solution.py:90
  319.8 10.1 %reshape.515 = f32[130,2,8192]{2,0,1:T(8,128)} reshape(f32[130,2,64,128]{3,2,0,1:T(8,128)} %fusion.28) | data formatting | bytes 17039360 | tf_op jit(solution)/shard_map/reshape | solution.py:91
  329.9 14.7 %copy.55 = f32[130,2,8192]{2,1,0:T(2,128)S(1)} copy(f32[130,2,8192]{2,0,1:T(8,128)} %reshape.515) | data formatting | bytes 17039360 | tf_op jit(solution)/shard_map/reshape | solution.py:91
  344.6 0.5 collective-permute-start.1
  345.2 12.8 %collective-permute-done.1 = f32[130,2,8192]{2,1,0:T(2,128)S(1)} collective-permute-done((f32[130,2,8192]{2,1,0:T(2,128)S(1)}, f32[130,2,8192]{2,1,0:T(2,128)S(1)}, u32[]{:S(2)}, u32[]{:S(2)}) %collective-permute-start.1) | collective-permute-done | bytes 8519712 | tf_op jit(solution)/shard_map/ppermute | solution.py:14
  358.1 17.0 %broadcast_select_fusion = f32[130,2,8192]{2,1,0:T(2,128)S(1)} fusion(f32[130,2,8192]{2,1,0:T(2,128)S(1)} %collective-permute-done.1, pred[]{:T(512)S(6)} %eq.38, f32[130,2,8192]{2,0,1:T(8,128)S(1)} %copy-done.2), kind=kLoop, calls=%fused_computation.22 | loop fusion | flops 2129920 | bytes 25559040 | tf_op jit(solution)/shard_map/jit(_where)/select_n | solution.py:150
  375.0 10.6 %multiply_subtract_fusion.1 = (f32[130,1,8192]{2,1,0:T(1,128)S(1)}, f32[130,1,8192]{2,1,0:T(1,128)S(1)}) fusion(f32[130,2,8192]{2,1,0:T(2,128)S(1)} %broadcast_select_fusion, f32[8192]{0:T(1024)S(1)} %get-tuple-element.44, f32[8192]{0:T(1024)S(1)} %get-tuple-element.45), kind=kLoop, calls=%fused_computation.38 | loop fusion | flops 6389760 | bytes 17104896 | tf_op jit(solution)/shard_map/sub | solution.py:61
  385.6 7.4 %broadcast_in_dim.28 = bf16[1,256,2,8192]{3,2,1,0:T(2,128)(2,1)} broadcast(bf16[]{:T(256)} %constant.133.clone.1), dimensions={} | broadcast | bytes 8388610 | tf_op jit(solution)/shard_map/broadcast_in_dim | solution.py:156
  393.1 24.6 %bitcast_dynamic-update-slice_fusion = bf16[1,256,2,8192]{3,2,1,0:T(2,128)(2,1)} fusion(bf16[1,256,2,8192]{3,2,1,0:T(2,128)(2,1)} %broadcast_in_dim.28, s32[]{:T(128)S(6)} %select_n.211, f32[130,1,8192]{2,1,0:T(1,128)S(1)} %get-tuple-element.12, f32[130,1,8192]{2,1,0:T(1,128)S(1)} %get-tuple-element.11, f32[]{:T(128)S(6)} %convert_element_type.214, ...), kind=kLoop, calls=%fused_computation.36 | loop fusion | flops 12779520 | bytes 29818888 | tf_op jit(solution)/shard_map/dynamic_update_slice | solution.py:157
  (35 shorter events, 2.7 us)
Async XLA Ops:
  0.0 2.7 copy-start
  19.8 199.0 %all-to-all-start = ((bf16[128,2,2,8192]{3,2,1,0:T(2,128)(2,1)}), bf16[128,2,2,8192]{3,2,1,0:T(2,128)(2,1)}, u32[]{:S(2)}, u32[]{:S(2)}) async-start(bf16[128,2,2,8192]{3,2,1,0:T(2,128)(2,1)} %copy.48), calls=%async_computation | async-start | bytes 16777216 | tf_op jit(solution)/shard_map/all_to_all | solution.py:129
  36.7 200.5 %copy-start.3 = (s32[128]{0:T(128)S(1)}, s32[128]{0:T(128)}, u32[]{:S(2)}) copy-start(s32[128]{0:T(128)} %param.10) | copy-start | bytes 1540
  36.7 201.1 %copy-start.4 = (f32[32]{0:T(128)S(1)}, f32[32]{0:T(128)}, u32[]{:S(2)}) copy-start(f32[32]{0:T(128)} %param.9) | copy-start | bytes 388
  230.6 13.8 %collective-permute-start = (bf16[130,2,8192]{2,1,0:T(2,128)(2,1)}, bf16[130,2,8192]{2,1,0:T(2,128)(2,1)}, u32[]{:S(2)}, u32[]{:S(2)}) collective-permute-start(bf16[130,2,8192]{2,1,0:T(2,128)(2,1)} %constant_dynamic-slice_fusion), channel_id=1, source_target_pairs={{0,1},{1,0},{2,3},{3,2},{4,5},{5,4},{6,7},{7,6},{8,9},{9,8},{10,11... | collective-permute-start | bytes 12779528 | tf_op jit(solution)/shard_map/ppermute | solution.py:14
  329.9 28.2 %copy-start.2 = (f32[130,2,8192]{2,0,1:T(8,128)S(1)}, f32[130,2,8192]{2,0,1:T(8,128)}, u32[]{:S(2)}) copy-start(f32[130,2,8192]{2,0,1:T(8,128)} %reshape.515) | copy-start | bytes 25559044
  344.6 13.4 %collective-permute-start.1 = (f32[130,2,8192]{2,1,0:T(2,128)S(1)}, f32[130,2,8192]{2,1,0:T(2,128)S(1)}, u32[]{:S(2)}, u32[]{:S(2)}) collective-permute-start(f32[130,2,8192]{2,1,0:T(2,128)S(1)} %copy.55), channel_id=1, source_target_pairs={{0,1},{1,0},{2,3},{3,2},{4,5},{5,4},{6,7},{7,6},{8,9},{9,8},{10,11... | collective-permute-start | bytes 25559048 | tf_op jit(solution)/shard_map/ppermute | solution.py:14
  393.1 24.6 %copy-start.1 = (bf16[2,2,48,8192]{3,2,1,0:T(8,128)(2,1)S(1)}, bf16[2,2,48,8192]{3,2,1,0:T(8,128)(2,1)}, u32[]{:S(2)}) copy-start(bf16[2,2,48,8192]{3,2,1,0:T(8,128)(2,1)} %param.6) | copy-start | bytes 9437188
where the time goes:
time: 426 us; the launch traced here: 418 us
  waiting for transfers between devices  194 us (46%)
  other arithmetic  101 us (24%)
  local copies, waits for them, and re-layouts  60.7 us (14%)
  matrix products  34.3 us (8%)
  starting transfers between devices  23.9 us (6%)
    all_to_all x1, waiting for transfers between devices, per_device(): lax.all_to_all(beams_local, 'sub', split_axis=0, concat_axis=1, tiled=True)  179 us
    sub x5, other arithmetic, rotate(): real_part * cosine - imag_part * sine  41 us
    reshape x2, local copies, waits for them, and re-layouts, inverse_dft(): return result_grid.reshape(row_count, 2, length)  24.8 us
    dynamic_update_slice x1, other arithmetic, per_device(): lax.dynamic_update_slice_in_dim(blank, result_window, window_start, 0)  24.6 us
    select_n x1, other arithmetic, per_device(): odd_part = jnp.where(section_index == 0, remote, partial_result)  17 us
    all_to_all x1, starting transfers between devices, per_device(): lax.all_to_all(beams_local, 'sub', split_axis=0, concat_axis=1, tiled=True)  16.9 us
    dot_general x1, matrix products, forward_dft(): jnp.einsum('rckq,cqdj->rdkj', partial_sums, second_table, precision=PRECISE)  16.6 us
    ppermute x2, waiting for transfers between devices, partner_2(): return lax.ppermute(value, axis, pairs)  15.3 us
  transfers between devices with their start and end apart: 3, of which 3 were waited for; matrix products, arithmetic and copies ran while one was open for 1% of the time, Pallas kernels for 0%

commit v1 on v0

v1 whole, which is shorter than its diff:
```python
import functools
import math

import jax
import jax.numpy as jnp
import numpy as np
from jax import lax
from jax.experimental import pallas as pl
from jax.experimental.pallas import tpu as pltpu
from jax.sharding import PartitionSpec as P

MESH = pl.DeviceIdType.MESH
NX, NZ, NY = 4, 8, 4
LENGTH = 16384
SIDE = 128
HALF = LENGTH // 2
QUARTER = HALF // 2
CHUNKS = NZ
OFFSETS = (4, 3, 5, 2, 6, 1, 7, 0)
LANES = 256


def chunk_offset(chunk):
    step = (chunk + 1) // 2
    return lax.rem(NZ // 2 + step * (1 - 2 * lax.rem(chunk, 2)) + NZ, NZ)


def split_table(table):
    high = table.astype(jnp.bfloat16)
    low = (table - high.astype(np.float64)).astype(jnp.bfloat16)
    return np.stack([high, low])


def dft_tables():
    index = np.arange(SIDE)
    angle = 2.0 * np.pi * (np.outer(index, index) % SIDE) / SIDE
    cosine, sine = np.cos(angle), np.sin(angle)
    first = np.block([[cosine, sine], [-sine, cosine]])
    second = np.block([[cosine, -sine], [sine, cosine]])
    third = np.block([[cosine, sine], [-sine, cosine]])
    fourth = np.empty((SIDE, 2, 2 * SIDE))
    fourth[:, 0] = np.concatenate([cosine, -sine], axis=1)
    fourth[:, 1] = np.concatenate([sine, cosine], axis=1)
    fourth = fourth.reshape(2 * SIDE, 2 * SIDE) / LENGTH
    dfts = np.stack([split_table(t) for t in (first, second, third, fourth)])
    twist = 2.0 * np.pi * np.outer(index, index) / LENGTH
    bins = index[:, None] + SIDE * np.where(index < SIDE // 2, index, index - SIDE)[None, :]
    planes = np.stack([np.cos(twist), np.sin(twist), (bins * bins).astype(np.float64)])
    return dfts, planes.astype(np.float32)


def turn_coefficients():
    grid = np.cos(np.pi * (np.arange(400) + 0.5) / 400) * 0.25 + 0.25
    x = np.sqrt(grid) * 0.5 / np.sqrt(0.5)
    square = x * x
    cosine = np.polynomial.chebyshev.Chebyshev.fit(square, np.cos(2 * np.pi * x), 6, domain=[0, 0.25])
    sine = np.polynomial.chebyshev.Chebyshev.fit(
        square, np.sin(2 * np.pi * x) / x, 6, domain=[0, 0.25]
    )
    power = np.polynomial.Polynomial
    return (
        [float(v) for v in cosine.convert(kind=power).coef],
        [float(v) for v in sine.convert(kind=power).coef],
    )


def horner(coefficients, x):
    total = coefficients[-1]
    for value in coefficients[-2::-1]:
        total = total * x + value
    return total


def split(value):
    high = value.astype(jnp.bfloat16)
    return high, (value - high.astype(jnp.float32)).astype(jnp.bfloat16)


def dot(left, right):
    return jnp.dot(left, right, preferred_element_type=jnp.float32)


def kernel(
    cosine_poly,
    sine_poly,
    weights,
    voltages,
    dfts,
    planes,
    dispersion,
    gathered,
    formed,
    arrived,
    grid,
    results,
    x_send,
    x_recv,
    z_send,
    z_recv,
    own_sem,
):
    me = lax.axis_index("sub")
    core = lax.axis_index("section")
    my_x = me // (NZ * NY)
    my_z = lax.rem(me // NY, NZ)
    my_y = lax.rem(me, NY)
    plane_start = my_x * (NZ * NY)

    barrier = pltpu.get_barrier_semaphore()

    def x_partner(step):
        other_x = lax.rem(my_x - step // 2 + NX, NX)
        other_core = lax.rem(core + lax.rem(step, 2), 2)
        return other_x, other_core

    def greet_x(step, carry):
        other_x, other_core = x_partner(step)
        pl.semaphore_signal(
            barrier, inc=1, device_id=((other_x * NZ + my_z) * NY + my_y, other_core), device_id_type=MESH
        )
        return carry

    def greet_plane(step, carry):
        other = lax.rem(my_z * NY + my_y + step // 2, NZ * NY)
        other_core = lax.rem(core + lax.rem(step, 2), 2)
        pl.semaphore_signal(
            barrier, inc=1, device_id=(plane_start + other, other_core), device_id_type=MESH
        )
        return carry

    lax.fori_loop(2, 2 * NX, greet_x, 0)
    lax.fori_loop(1, 2 * NZ * NY, greet_plane, 0)

    tiles = QUARTER // LANES

    def form(step, carry):
        local = step // tiles
        start = pl.multiple_of(lax.rem(step, tiles) * LANES, LANES)
        parts = []
        for quarter in range(2):
            block = voltages[local, :, pl.ds(quarter * QUARTER + start, LANES)]
            product = dot(weights[local], block)
            parts.append(product.reshape(CHUNKS * NX, 8, LANES))
        both = jnp.concatenate(parts, axis=1).astype(jnp.bfloat16)
        formed[pl.ds(local * (CHUNKS * NX), CHUNKS * NX), :, pl.ds(start, LANES)] = both
        return carry

    lax.fori_loop(0, 2 * tiles, form, 0)

    pl.semaphore_wait(barrier, 2 * NX - 2 + 2 * NZ * NY - 1)

    def x_copy(chunk, step):
        other_x, other_core = x_partner(step)
        return pltpu.make_async_remote_copy(
            src_ref=formed.at[(other_core * CHUNKS + chunk) * NX + other_x],
            dst_ref=arrived.at[chunk, step],
            send_sem=x_send.at[chunk],
            recv_sem=x_recv.at[chunk],
            device_id=((other_x * NZ + my_z) * NY + my_y, other_core),
            device_id_type=MESH,
        )

    def own_copy(chunk):
        return pltpu.make_async_copy(
            formed.at[(core * CHUNKS + chunk) * NX + my_x], arrived.at[chunk, 0], own_sem.at[chunk]
        )

    def start_x(chunk):
        def one(step, carry):
            x_copy(chunk, step).start()
            return carry

        lax.fori_loop(1, 2 * NX, one, 0)
        own_copy(chunk).start()

    def wait_x_sent(chunk):
        pltpu.make_async_copy(
            formed.at[pl.ds(0, 2 * NX - 1)], formed.at[pl.ds(0, 2 * NX - 1)], x_send.at[chunk]
        ).wait()

    start_x(0)
    start_x(1)

    slot = (my_z * NY + my_y) * 2 + core

    def do_chunk(chunk, carry):
        pltpu.make_async_copy(
            arrived.at[chunk, pl.ds(1, 2 * NX - 1)],
            arrived.at[chunk, pl.ds(1, 2 * NX - 1)],
            x_recv.at[chunk],
        ).wait()
        own_copy(chunk).wait()

        @pl.when(chunk < CHUNKS - 2)
        def _():
            start_x(chunk + 2)

        def fold(step, carry):
            group = step // 2
            other = lax.rem(step, 2)
            half = lax.rem(core + other, 2)

            def lane_tile(index, carry):
                lanes = pl.ds(pl.multiple_of(index * SIDE, SIDE), SIDE)
                near = arrived[chunk, group * 2 + other, :, lanes].astype(jnp.float32)
                far = arrived[chunk, group * 2 + 4 + other, :, lanes].astype(jnp.float32)
                total = near + far
                row = half * (SIDE // 2) + index
                grid[group, pl.ds(row, 8, stride=SIDE), :] = total[:8]
                grid[group, pl.ds(row + QUARTER // SIDE, 8, stride=SIDE), :] = total[8:]
                return carry

            lax.fori_loop(0, QUARTER // SIDE, lane_tile, 0)
            return carry

        lax.fori_loop(0, 4, fold, 0)

        def transform(beam, carry):
            rows = pl.ds(pl.multiple_of(beam * 2 * SIDE, 2 * SIDE), 2 * SIDE)
            series = jnp.concatenate([grid[0, rows, :], grid[1, rows, :]], axis=1).astype(jnp.bfloat16)
            stage = dot(dfts[0, 0], series) + dot(dfts[0, 1], series)
            cosine, sine = planes[0], planes[1]
            turned = []
            for group in range(2):
                lanes = slice(group * SIDE, (group + 1) * SIDE)
                real, imag = stage[:SIDE, lanes], stage[SIDE:, lanes]
                turned.append(
                    jnp.concatenate([real * cosine + imag * sine, imag * cosine - real * sine], axis=1)
                )
            high, low = split(jnp.concatenate(turned, axis=0))
            stage = dot(high, dfts[1, 0]) + dot(high, dfts[1, 1]) + dot(low, dfts[1, 0])
            turned = []
            for group in range(2):
                rows_of = slice(group * SIDE, (group + 1) * SIDE)
                real, imag = stage[rows_of, :SIDE], stage[rows_of, SIDE:]
                turns = dispersion[(chunk * NY + beam) * 2 + group] * planes[2]
                turns = turns - jnp.round(turns)
                square = turns * turns
                chirp_cos = horner(cosine_poly, square)
                chirp_sin = horner(sine_poly, square) * turns
                turned.append(
                    jnp.concatenate(
                        [real * chirp_cos - imag * chirp_sin, real * chirp_sin + imag * chirp_cos], axis=1
                    )
                )
            high, low = split(jnp.concatenate(turned, axis=0))
            stage = dot(high, dfts[2, 0]) + dot(high, dfts[2, 1]) + dot(low, dfts[2, 0])
            turned = []
            for group in range(2):
                rows_of = slice(group * SIDE, (group + 1) * SIDE)
                real, imag = stage[rows_of, :SIDE], stage[rows_of, SIDE:]
                turned.append(
                    jnp.concatenate([real * cosine - imag * sine, real * sine + imag * cosine], axis=0)
                )
            high, low = split(jnp.concatenate(turned, axis=1))
            final = dot(dfts[3, 0], high) + dot(dfts[3, 1], high) + dot(dfts[3, 0], low)
            final = final.astype(jnp.bfloat16)
            for section in range(2):
                message = (chunk * NY + beam) * 2 + section
                for group in range(2):
                    parity = lax.rem(my_x + group, 2)
                    results[message, parity] = final[
                        section * SIDE : (section + 1) * SIDE, group * SIDE : (group + 1) * SIDE
                    ]
            return carry

        lax.fori_loop(0, NY, transform, 0)

        offset = chunk_offset(chunk)

        def send(step, carry):
            beam = step // 2
            section = lax.rem(step, 2)
            up = lax.rem(my_z + offset, NZ)
            down = lax.rem(my_z - offset + NZ, NZ)
            other_z = jnp.where(beam < NY // 2, up, down)
            target = plane_start + other_z * NY + beam
            message = chunk * (NY * 2) + step
            own = jnp.logical_and(target == me, section == core)

            @pl.when(own)
            def _():
                pltpu.make_async_copy(
                    results.at[message], gathered.at[:, slot], own_sem.at[CHUNKS]
                ).start()

            @pl.when(jnp.logical_not(own))
            def _():
                pltpu.make_async_remote_copy(
                    src_ref=results.at[message],
                    dst_ref=gathered.at[:, slot],
                    send_sem=z_send,
                    recv_sem=z_recv,
                    device_id=(target, section),
                    device_id_type=MESH,
                ).start()

            return carry

        lax.fori_loop(0, 2 * NY, send, 0)
        return carry

    lax.fori_loop(0, CHUNKS, do_chunk, 0)

    for chunk in range(CHUNKS):
        wait_x_sent(chunk)
    others = 2 * NZ * NY - 1
    pltpu.make_async_copy(
        results.at[0], gathered.at[:, slot], own_sem.at[CHUNKS]
    ).wait()
    pltpu.make_async_copy(results.at[pl.ds(0, others)], results.at[pl.ds(0, others)], z_send).wait()
    pltpu.make_async_copy(
        gathered.at[:, pl.ds(0, others)], gathered.at[:, pl.ds(0, others)], z_recv
    ).wait()


def in_chunk_order(values, my_z):
    grid = values.reshape((NX, NZ, 2, NY // 2) + values.shape[1:])
    doubled = jnp.concatenate([grid, grid], axis=1)
    turned = lax.dynamic_slice_in_dim(doubled, my_z, NZ, axis=1)
    up = jnp.stack([turned[:, k, 0] for k in OFFSETS])
    down = jnp.stack([turned[:, (NZ - k) % NZ, 1] for k in OFFSETS])
    return jnp.concatenate([up, down], axis=2)


def row_frequency(row_ids, subbands):
    return 1.0 + (row_ids.astype(jnp.float32) + 0.5) / subbands


def per_device(voltages, delay_table, delay_index, dm_table, dm_index, range_bounds):
    beams = delay_index.shape[0]
    stations = voltages.shape[2]
    subbands = voltages.shape[0] * lax.axis_size("sub")
    sub_index = lax.axis_index("sub")
    core = lax.axis_index("section")
    my_x = sub_index // (NZ * NY)
    my_z = lax.rem(sub_index // NY, NZ)
    own_beam = sub_index

    ordered_delay = in_chunk_order(delay_index, my_z).reshape(beams, stations)
    ordered_bounds = in_chunk_order(range_bounds, my_z).reshape(beams, 2)
    ordered_entry = in_chunk_order(dm_index, my_z)

    picked = ordered_delay[:, :, None] == jnp.arange(delay_table.shape[0])[None, None, :]
    delays = jnp.sum(jnp.where(picked, delay_table, 0.0), axis=-1)
    local_ids = sub_index * 2 + jnp.arange(2)
    local_freq = row_frequency(local_ids, subbands)
    angles = (2.0 * math.pi * delays)[None] * local_freq[:, None, None]
    scaling = 1.0 / math.sqrt(stations)
    w_real = (jnp.cos(angles) * scaling).astype(jnp.bfloat16)
    w_imag = (-jnp.sin(angles) * scaling).astype(jnp.bfloat16)
    live = (local_ids[:, None] >= ordered_bounds[None, :, 0]) & (
        local_ids[:, None] < ordered_bounds[None, :, 1]
    )
    blank = jnp.zeros((), jnp.bfloat16)
    w_real = jnp.where(live[:, :, None], w_real, blank)
    w_imag = jnp.where(live[:, :, None], w_imag, blank)
    weights = jnp.stack(
        [jnp.concatenate([w_real, -w_imag], axis=2), jnp.concatenate([w_imag, w_real], axis=2)], axis=2
    ).reshape(2, 2 * beams, 2 * stations)

    entry = lax.dynamic_index_in_dim(ordered_entry, my_x, axis=1, keepdims=False).reshape(CHUNKS * NY)
    bounds = lax.dynamic_index_in_dim(
        ordered_bounds.reshape(CHUNKS, NX, NY, 2), my_x, axis=1, keepdims=False
    ).reshape(CHUNKS * NY, 2)
    strength = jnp.sum(
        jnp.where(entry[:, None] == jnp.arange(dm_table.shape[0])[None, :], dm_table, 0.0), axis=-1
    )
    in_plane = lax.rem(sub_index, NZ * NY)
    parity = lax.rem(my_x + jnp.arange(2), 2)
    low_row = parity * (subbands // 4) + 2 * in_plane + core
    high_row = low_row + subbands // 2
    high_live = (high_row[None, :] >= bounds[:, :1]) & (high_row[None, :] < bounds[:, 1:])
    freq = row_frequency(jnp.where(high_live, high_row[None, :], low_row[None, :]), subbands)
    dispersion = (0.5 * strength[:, None] / (LENGTH * (freq * freq * freq))).reshape(-1)

    dfts, planes = dft_tables()
    cosine_poly, sine_poly = turn_coefficients()
    vmem = pl.BlockSpec(memory_space=pltpu.VMEM)
    gathered = pl.pallas_call(
        functools.partial(kernel, cosine_poly, sine_poly),
        out_shape=jax.ShapeDtypeStruct((2, NZ * NY * 2, SIDE, SIDE), jnp.bfloat16),
        in_specs=[vmem, vmem, vmem, vmem, pl.BlockSpec(memory_space=pltpu.SMEM)],
        out_specs=pl.BlockSpec(memory_space=pl.ANY),
        scratch_shapes=[
            pltpu.VMEM((2 * CHUNKS * NX, 16, QUARTER), jnp.bfloat16),
            pltpu.VMEM((CHUNKS, 2 * NX, 16, QUARTER), jnp.bfloat16),
            pltpu.VMEM((2, 2 * NY * SIDE, SIDE), jnp.float32),
            pltpu.VMEM((CHUNKS * NY * 2, 2, SIDE, SIDE), jnp.bfloat16),
            pltpu.SemaphoreType.DMA((CHUNKS,)),
            pltpu.SemaphoreType.DMA((CHUNKS,)),
            pltpu.SemaphoreType.DMA,
            pltpu.SemaphoreType.DMA,
            pltpu.SemaphoreType.DMA((CHUNKS + 1,)),
        ],
        compiler_params=pltpu.CompilerParams(
            collective_id=0, has_side_effects=True, vmem_limit_bytes=56 * 1024 * 1024
        ),
        name="beams",
    )(
        weights,
        voltages.reshape(2, 2 * stations, HALF),
        jnp.asarray(dfts),
        jnp.asarray(planes),
        dispersion,
    )

    rows = gathered.reshape(subbands // 2, SIDE // 2, 2, SIDE)
    rows = jnp.transpose(rows, (0, 2, 1, 3)).reshape(1, subbands // 2, 2, HALF)
    own_bounds = lax.dynamic_index_in_dim(range_bounds, own_beam, keepdims=False)
    ids = jnp.arange(subbands).reshape(2, subbands // 2, 1, 1)
    alive = (ids >= own_bounds[0]) & (ids < own_bounds[1])
    placed = jnp.where(alive, rows, jnp.zeros((), jnp.bfloat16))
    return placed.reshape(1, subbands, 2, HALF)


def solution(mesh):
    return jax.shard_map(
        per_device,
        mesh=mesh,
        in_specs=(P("sub", None, None, "section"), P(), P(), P(), P(), P()),
        out_specs=P("sub", None, None, "section"),
        check_vma=False,
    )
```

time: 426 us -> 170 us (0.40); the launches traced: 418 us -> 169 us
  waiting for transfers between devices: 194 us -> 0 us
  Pallas kernels: 0 us -> 138 us
  other arithmetic: 101 us -> 14.2 us
  local copies, waits for them, and re-layouts: 60.7 us -> 17.1 us
  matrix products: 34.3 us -> 0 us
  starting transfers between devices: 23.9 us -> 0 us
    all_to_all x1 -> x0, waiting for transfers between devices: 179 us -> none  [per_device(): lax.all_to_all(beams_local, 'sub', split_axis=0, concat_axis=1, tiled=True)]
    pallas_call x0 -> x1, Pallas kernels: none -> 138 us  [per_device(): pl.pallas_call(functools.partial(kernel, cosine_poly, sine_poly), out_sha...]
    sub x5 -> x0, other arithmetic: 41 us -> none  [rotate(): real_part * cosine - imag_part * sine]
    dot_general x5 -> x0, matrix products: 34.3 us -> none  [the longest x1 16.6 us: forward_dft(): jnp.einsum('rckq,cqdj->rdkj', partial_sums, second_table, precision=PRECISE)]
    dynamic_update_slice x1 -> x0, other arithmetic: 24.6 us -> none  [per_device(): lax.dynamic_update_slice_in_dim(blank, result_window, window_start, 0)]
    reshape x2 -> x6, local copies, waits for them, and re-layouts: 24.8 us -> 2.15 us  [the longest x4 1.95 us: in_chunk_order(): grid = values.reshape((NX, NZ, 2, NY // 2) + values.shape[1:])]
    all_to_all x1 -> x0, starting transfers between devices: 16.9 us -> none  [per_device(): lax.all_to_all(beams_local, 'sub', split_axis=0, concat_axis=1, tiled=True)]
    ppermute x2 -> x0, waiting for transfers between devices: 15.3 us -> none  [partner_2(): return lax.ppermute(value, axis, pairs)]
  transfers between devices with their start and end apart: 3 -> 0, of which waited for: 3 -> 0; matrix products, arithmetic and copies ran while one was open for 1% -> 0% of each run, Pallas kernels for 0% -> 0%
where the time goes in v1:
time: 170 us; the launch traced here: 169 us
  Pallas kernels  138 us (81%)
  local copies, waits for them, and re-layouts  17.1 us (10%)
  other arithmetic  14.2 us (8%)
    pallas_call x1, Pallas kernels, per_device(): pl.pallas_call(functools.partial(kernel, cosine_poly, sine_poly), out_sha...  138 us
    select_n x1, other arithmetic, per_device(): placed = jnp.where(alive, rows, jnp.zeros((), jnp.bfloat16))  9.19 us
    broadcast_in_dim x1, local copies, waits for them, and re-layouts, per_device(): placed = jnp.where(alive, rows, jnp.zeros((), jnp.bfloat16))  8.29 us

profile of v1, /device:TPU:1, one launch (start us, length us, event | category | flops | bytes accessed | tf_op | source)
XLA Modules:
  0.0 169.5 jit_solution(12592926021404825394)
XLA Ops:
  0.0 0.8 constant_dynamic-slice_fusion
  0.8 0.6 fusion.19
  1.4 1.3 and_bitcast_fusion
  2.8 0.1 ge.58
  2.9 0.1 broadcast_in_dim.93
  3.0 0.8 reshape.192
  3.8 0.1 copy.162
  3.9 0.1 dynamic-slice_add_fusion.2
  4.0 0.7 slice_reduce_fusion.24
  4.9 0.3 fusion.9
  5.3 0.8 select_reduce_fusion.1
  6.2 0.1 div.43
  6.3 0.8 copy.144
  7.1 0.1 fusion
  7.5 1.1 select_reduce_fusion
  8.6 0.8 reshape.187
  9.5 0.2 copy.141
  9.6 0.1 dynamic-slice_add_fusion.1
  9.8 1.3 slice_reduce_fusion.8
  11.2 0.1 fusion.6
  11.3 0.2 copy.164
  11.5 0.1 reshape.193
  11.6 0.2 copy.143
  11.8 0.1 reshape.188
  12.1 0.1 ge.61
  12.3 0.1 lt.70
  12.4 0.5 fusion.11.dispersion
  13.0 0.3 fusion.17
  13.3 0.8 copy.161
  14.1 137.9 %beams.1 = bf16[2,64,128,128]{3,2,1,0:T(8,128)(2,1)} custom-call(bf16[2,256,96]{2,1,0:T(8,128)(2,1)} %bitcast.197, bf16[2,96,8192]{2,1,0:T(8,128)(2,1)} %bitcast.196, bf16[4,2,256,256]{3,2,1,0:T(8,128)(2,1)} %constant.90.clone.dfts, f32[3,128,128]{2,1,0:T(8,128)} %constant.91.clone.planes, f32[64]{0:T(128)} %fusion.11.dispersion), custom_call_target="tpu_custom_call" | custom-call | tf_op jit(solution)/shard_map/beams/pallas_call | solution.py:380
  152.0 8.3 %broadcast_in_dim.95 = bf16[2,128,2,8192]{3,2,1,0:T(2,128)(2,1)S(1)} broadcast(bf16[128,2,8192]{2,1,0:T(2,128)(2,1)} %bitcast.195), dimensions={1,2,3} | broadcast | bytes 12582912 | tf_op jit(solution)/shard_map/jit(_where)/broadcast_in_dim | solution.py:413
  160.3 9.2 %broadcast_select_fusion = bf16[1,256,2,8192]{3,2,1,0:T(2,128)(2,1)} fusion(pred[256]{0:T(512)(128)(4,1)S(1)} %and_bitcast_fusion, bf16[1,256,2,8192]{3,2,1,0:T(2,128)(2,1)S(1)} %bitcast.194), kind=kLoop, calls=%fused_computation | loop fusion | flops 4194304 | bytes 16777472 | tf_op jit(solution)/shard_map/jit(_where)/select_n | solution.py:413
  (60 shorter events, 0.9 us)

commit v2 on v1

v2 whole, which is shorter than its diff:
```python
import functools
import math

import jax
import jax.numpy as jnp
import numpy as np
from jax import lax
from jax.experimental import pallas as pl
from jax.experimental.pallas import tpu as pltpu
from jax.sharding import PartitionSpec as P

MESH = pl.DeviceIdType.MESH
NX, NZ, NY = 4, 8, 4
LENGTH = 16384
SIDE = 128
HALF = LENGTH // 2
PIECES = 4
PIECE = HALF // PIECES
PAIR = 2
CHUNKS = NZ * NY // PAIR
AHEAD = 3
LANES = 256


def chunk_offset(chunk):
    index = chunk // 2
    step = (index + 1) // 2
    return (NZ // 2 + step * (1 - 2 * (index % 2)) + NZ) % NZ


def split_table(table):
    high = table.astype(jnp.bfloat16)
    low = (table - high.astype(np.float64)).astype(jnp.bfloat16)
    return np.stack([high, low])


def dft_tables():
    index = np.arange(SIDE)
    angle = 2.0 * np.pi * (np.outer(index, index) % SIDE) / SIDE
    cosine, sine = np.cos(angle), np.sin(angle)
    first = np.block([[cosine, sine], [-sine, cosine]])
    first = first.reshape(2 * SIDE, 2, 2, 2, 2, PIECE // SIDE)
    first = first.transpose(0, 1, 4, 2, 3, 5).reshape(2 * SIDE, 2 * SIDE)
    second = np.block([[cosine, -sine], [sine, cosine]])
    third = np.block([[cosine, sine], [-sine, cosine]])
    fourth = np.empty((SIDE, 2, 2 * SIDE))
    fourth[:, 0] = np.concatenate([cosine, -sine], axis=1)
    fourth[:, 1] = np.concatenate([sine, cosine], axis=1)
    fourth = fourth.reshape(2 * SIDE, 2 * SIDE) / LENGTH
    dfts = np.stack([split_table(t) for t in (first, second, third, fourth)])
    twist = 2.0 * np.pi * np.outer(index, index) / LENGTH
    bins = index[:, None] + SIDE * np.where(index < SIDE // 2, index, index - SIDE)[None, :]
    planes = np.stack([np.cos(twist), np.sin(twist), (bins * bins).astype(np.float64)])
    return dfts, planes.astype(np.float32)


def turn_coefficients():
    grid = np.cos(np.pi * (np.arange(400) + 0.5) / 400) * 0.25 + 0.25
    x = np.sqrt(grid) * 0.5 / np.sqrt(0.5)
    square = x * x
    cosine = np.polynomial.chebyshev.Chebyshev.fit(square, np.cos(2 * np.pi * x), 6, domain=[0, 0.25])
    sine = np.polynomial.chebyshev.Chebyshev.fit(
        square, np.sin(2 * np.pi * x) / x, 6, domain=[0, 0.25]
    )
    power = np.polynomial.Polynomial
    return (
        [float(v) for v in cosine.convert(kind=power).coef],
        [float(v) for v in sine.convert(kind=power).coef],
    )


def horner(coefficients, x):
    total = coefficients[-1]
    for value in coefficients[-2::-1]:
        total = total * x + value
    return total


def split(value):
    high = value.astype(jnp.bfloat16)
    return high, (value - high.astype(jnp.float32)).astype(jnp.bfloat16)


def dot(left, right):
    return jnp.dot(left, right, preferred_element_type=jnp.float32)


def turn_cos_sin(turns, cosine_poly, sine_poly):
    turns = turns - jnp.round(turns)
    square = turns * turns
    return horner(cosine_poly, square), horner(sine_poly, square) * turns


def kernel(
    cosine_poly,
    sine_poly,
    delay_table,
    dm_table,
    dm_index,
    bounds_scalar,
    cubes,
    delay_index,
    bounds,
    voltages,
    dfts,
    planes,
    gathered,
    weights,
    formed,
    arrived,
    grid,
    results,
    x_send,
    x_recv,
    z_send,
    z_recv,
    own_sem,
):
    me = lax.axis_index("sub")
    core = lax.axis_index("section")
    my_x = me // (NZ * NY)
    my_z = lax.rem(me // NY, NZ)
    my_y = lax.rem(me, NY)
    plane_start = my_x * (NZ * NY)

    barrier = pltpu.get_barrier_semaphore()

    def x_partner(step):
        other_x = lax.rem(my_x - step // 2 + NX, NX)
        other_core = lax.rem(core + lax.rem(step, 2), 2)
        return other_x, other_core

    def greet_x(step, carry):
        other_x, other_core = x_partner(step)
        pl.semaphore_signal(
            barrier, inc=1, device_id=((other_x * NZ + my_z) * NY + my_y, other_core), device_id_type=MESH
        )
        return carry

    def greet_plane(step, carry):
        other = lax.rem(my_z * NY + my_y + step // 2, NZ * NY)
        other_core = lax.rem(core + lax.rem(step, 2), 2)
        pl.semaphore_signal(
            barrier, inc=1, device_id=(plane_start + other, other_core), device_id_type=MESH
        )
        return carry

    lax.fori_loop(2, 2 * NX, greet_x, 0)
    lax.fori_loop(1, 2 * NZ * NY, greet_plane, 0)

    beams = NX * NZ * NY
    stations = delay_index.shape[0]
    subbands = 2 * beams

    entries = delay_index[...]

    def look_up(entry, total):
        return jnp.where(entries == entry, delay_table[entry], total)

    delays = lax.fori_loop(
        0, delay_table.shape[0], look_up, jnp.zeros((stations, beams), jnp.float32), unroll=8
    )
    row = lax.broadcasted_iota(jnp.int32, (CHUNKS * NX * 8, 1), 0)
    row_chunk = row // (NX * 8)
    row_pair = (row // 2) % PAIR
    row_z = (my_z + (1 - 2 * row_pair) * chunk_offset(row_chunk) + NZ) % NZ
    row_beam = ((row // 8) % NX) * (NZ * NY) + row_z * NY + PAIR * row_pair + row_chunk % 2
    column = lax.broadcasted_iota(jnp.int32, (CHUNKS * NX * 8, 2 * beams), 1)
    chosen = jnp.where(column == (row % 2) * beams + row_beam, 1.0, 0.0).astype(jnp.bfloat16)
    piece_of_row = (row // 4) % 2
    piece_of_lane = lax.broadcasted_iota(jnp.int32, (CHUNKS * NX * 8, 4 * stations), 1) // (2 * stations)
    scaling = 1.0 / math.sqrt(stations)
    for local in range(2):
        subband = 2 * me + local
        freq = 1.0 + (subband.astype(jnp.float32) + 0.5) * (1.0 / subbands)
        cosine, sine = turn_cos_sin(delays * freq, cosine_poly, sine_poly)
        live = jnp.logical_and(bounds[0:1, :] <= subband, bounds[1:2, :] > subband)
        cosine = jnp.where(live, cosine * scaling, 0.0)
        sine = jnp.where(live, sine * scaling, 0.0)
        both = jnp.concatenate(
            [
                jnp.concatenate([cosine, -sine], axis=1),
                jnp.concatenate([sine, cosine], axis=1),
            ],
            axis=0,
        )
        source = jnp.concatenate([both, both], axis=0).astype(jnp.bfloat16)
        placed = lax.dot_general(
            chosen, source, (((1,), (1,)), ((), ())), preferred_element_type=jnp.float32
        )
        weights[local] = jnp.where(piece_of_row == piece_of_lane, placed, 0.0).astype(jnp.bfloat16)

    tiles = PIECE // LANES

    def form(step, carry):
        local = step // tiles
        start = lax.rem(step, tiles) * LANES
        parts = []
        for couple in range(2):
            blocks = [
                voltages[
                    local, :, pl.ds(pl.multiple_of((couple * 2 + piece) * PIECE + start, LANES), LANES)
                ]
                for piece in range(2)
            ]
            product = dot(weights[local], jnp.concatenate(blocks, axis=0))
            parts.append(product.reshape(CHUNKS * NX, 8, LANES))
        both = jnp.concatenate(parts, axis=1).astype(jnp.bfloat16)
        formed[
            pl.ds(local * (CHUNKS * NX), CHUNKS * NX), :, pl.ds(pl.multiple_of(start, LANES), LANES)
        ] = both
        return carry

    lax.fori_loop(0, 2 * tiles, form, 0)

    pl.semaphore_wait(barrier, 2 * NX - 2 + 2 * NZ * NY - 1)

    def x_copy(chunk, step):
        other_x, other_core = x_partner(step)
        return pltpu.make_async_remote_copy(
            src_ref=formed.at[(other_core * CHUNKS + chunk) * NX + other_x],
            dst_ref=arrived.at[chunk, step],
            send_sem=x_send.at[chunk],
            recv_sem=x_recv.at[chunk],
            device_id=((other_x * NZ + my_z) * NY + my_y, other_core),
            device_id_type=MESH,
        )

    def own_copy(chunk):
        return pltpu.make_async_copy(
            formed.at[(core * CHUNKS + chunk) * NX + my_x], arrived.at[chunk, 0], own_sem.at[chunk]
        )

    def start_x(chunk):
        def one(step, carry):
            x_copy(chunk, step).start()
            return carry

        lax.fori_loop(1, 2 * NX, one, 0)
        own_copy(chunk).start()

    def wait_x_sent(chunk):
        pltpu.make_async_copy(
            formed.at[pl.ds(0, 2 * NX - 1)], formed.at[pl.ds(0, 2 * NX - 1)], x_send.at[chunk]
        ).wait()

    for chunk in range(AHEAD):
        start_x(chunk)

    slot = (my_z * NY + my_y) * 2 + core

    def do_chunk(chunk, carry):
        pltpu.make_async_copy(
            arrived.at[chunk, pl.ds(1, 2 * NX - 1)],
            arrived.at[chunk, pl.ds(1, 2 * NX - 1)],
            x_recv.at[chunk],
        ).wait()
        own_copy(chunk).wait()

        @pl.when(chunk < CHUNKS - AHEAD)
        def _():
            start_x(chunk + AHEAD)

        offset = chunk_offset(chunk)

        def fold(step, carry):
            group = step // 2
            other = lax.rem(step, 2)
            half = lax.rem(core + other, 2)

            def lane_tile(index, carry):
                lanes = pl.ds(pl.multiple_of(index * SIDE, SIDE), SIDE)
                near = arrived[chunk, group * 2 + other, :, lanes].astype(jnp.float32)
                far = arrived[chunk, group * 2 + 4 + other, :, lanes].astype(jnp.float32)
                total = near + far
                row = half * (SIDE // 4) + index
                grid[group, pl.ds(row, 8, stride=SIDE // 2), :] = total[:8]
                grid[group, pl.ds(row + SIDE // 8, 8, stride=SIDE // 2), :] = total[8:]
                return carry

            lax.fori_loop(0, PIECE // SIDE, lane_tile, 0, unroll=4)
            return carry

        lax.fori_loop(0, 4, fold, 0)

        def transform(beam, carry):
            other_z = lax.rem(my_z + (1 - 2 * beam) * offset + NZ, NZ)
            other_y = PAIR * beam + lax.rem(chunk, 2)
            beam_id = plane_start + other_z * NY + other_y
            strength = dm_table[dm_index[beam_id]]
            series = []
            for group in range(2):
                pieces = [
                    grid[
                        group,
                        pl.ds(pl.multiple_of((piece * 4 + beam * 2) * (SIDE // 2) + part * (SIDE // 2), SIDE // 2), SIDE // 2),
                        :,
                    ]
                    for part in range(2)
                    for piece in range(2)
                ]
                series.append(jnp.concatenate(pieces, axis=0))
            series = jnp.concatenate(series, axis=1).astype(jnp.bfloat16)
            stage = dot(dfts[0, 0], series) + dot(dfts[0, 1], series)
            cosine, sine = planes[0], planes[1]
            turned = []
            for group in range(2):
                lanes = slice(group * SIDE, (group + 1) * SIDE)
                real, imag = stage[:SIDE, lanes], stage[SIDE:, lanes]
                turned.append(
                    jnp.concatenate([real * cosine + imag * sine, imag * cosine - real * sine], axis=1)
                )
            high, low = split(jnp.concatenate(turned, axis=0))
            stage = dot(high, dfts[1, 0]) + dot(high, dfts[1, 1]) + dot(low, dfts[1, 0])
            turned = []
            for group in range(2):
                rows_of = slice(group * SIDE, (group + 1) * SIDE)
                real, imag = stage[rows_of, :SIDE], stage[rows_of, SIDE:]
                low_row = lax.rem(my_x + group, 2) * (subbands // 4) + 2 * (my_z * NY + my_y) + core
                high_row = low_row + subbands // 2
                is_high = jnp.logical_and(
                    bounds_scalar[0, beam_id] <= high_row, bounds_scalar[1, beam_id] > high_row
                )
                dispersion = strength * cubes[jnp.where(is_high, high_row, low_row)]
                chirp_cos, chirp_sin = turn_cos_sin(dispersion * planes[2], cosine_poly, sine_poly)
                turned.append(
                    jnp.concatenate(
                        [real * chirp_cos - imag * chirp_sin, real * chirp_sin + imag * chirp_cos], axis=1
                    )
                )
            high, low = split(jnp.concatenate(turned, axis=0))
            stage = dot(high, dfts[2, 0]) + dot(high, dfts[2, 1]) + dot(low, dfts[2, 0])
            turned = []
            for group in range(2):
                rows_of = slice(group * SIDE, (group + 1) * SIDE)
                real, imag = stage[rows_of, :SIDE], stage[rows_of, SIDE:]
                turned.append(
                    jnp.concatenate([real * cosine - imag * sine, real * sine + imag * cosine], axis=0)
                )
            high, low = split(jnp.concatenate(turned, axis=1))
            final = dot(dfts[3, 0], high) + dot(dfts[3, 1], high) + dot(dfts[3, 0], low)
            final = final.astype(jnp.bfloat16)
            for section in range(2):
                message = (chunk * PAIR + beam) * 2 + section
                for group in range(2):
                    parity = lax.rem(my_x + group, 2)
                    results[message, parity] = final[
                        section * SIDE : (section + 1) * SIDE, group * SIDE : (group + 1) * SIDE
                    ]

            def send(section, carry):
                message = (chunk * PAIR + beam) * 2 + section
                own = jnp.logical_and(beam_id == me, section == core)

                @pl.when(own)
                def _():
                    pltpu.make_async_copy(
                        results.at[message], gathered.at[:, slot], own_sem.at[CHUNKS]
                    ).start()

                @pl.when(jnp.logical_not(own))
                def _():
                    pltpu.make_async_remote_copy(
                        src_ref=results.at[message],
                        dst_ref=gathered.at[:, slot],
                        send_sem=z_send,
                        recv_sem=z_recv,
                        device_id=(beam_id, section),
                        device_id_type=MESH,
                    ).start()

                return carry

            lax.fori_loop(0, 2, send, 0)
            return carry

        lax.fori_loop(0, PAIR, transform, 0)
        return carry

    lax.fori_loop(0, CHUNKS, do_chunk, 0)

    for chunk in range(CHUNKS):
        wait_x_sent(chunk)
    others = 2 * NZ * NY - 1
    pltpu.make_async_copy(
        results.at[0], gathered.at[:, slot], own_sem.at[CHUNKS]
    ).wait()
    pltpu.make_async_copy(results.at[pl.ds(0, others)], results.at[pl.ds(0, others)], z_send).wait()
    pltpu.make_async_copy(
        gathered.at[:, pl.ds(0, others)], gathered.at[:, pl.ds(0, others)], z_recv
    ).wait()


BLOCK = 16


def place_kernel(bounds, gathered, placed):
    me = lax.axis_index("sub")
    start, end = bounds[0, me], bounds[1, me]
    rows = placed.shape[1] * pl.num_programs(0)
    first = pl.program_id(0) * BLOCK
    for high in range(2):
        row = high * rows + first + lax.broadcasted_iota(jnp.int32, (BLOCK, 1, 1), 0)
        live = jnp.logical_and(row >= start, row < end)
        value = jnp.where(live, gathered[...].astype(jnp.float32), 0.0)
        placed[high] = value.astype(jnp.bfloat16)


def per_device(voltages, delay_table, delay_index, dm_table, dm_index, range_bounds):
    stations = voltages.shape[2]
    subbands = voltages.shape[0] * lax.axis_size("sub")
    frequency = 1.0 + (np.arange(subbands) + 0.5) / subbands
    cubes = (0.5 / (LENGTH * frequency**3)).astype(np.float32)
    dfts, planes = dft_tables()
    cosine_poly, sine_poly = turn_coefficients()
    vmem = pl.BlockSpec(memory_space=pltpu.VMEM)
    smem = pl.BlockSpec(memory_space=pltpu.SMEM)
    bounds = range_bounds.T
    gathered = pl.pallas_call(
        functools.partial(kernel, cosine_poly, sine_poly),
        out_shape=jax.ShapeDtypeStruct((2, NZ * NY * 2, SIDE, SIDE), jnp.bfloat16),
        in_specs=[smem] * 5 + [vmem] * 5,
        out_specs=pl.BlockSpec(memory_space=pl.ANY),
        scratch_shapes=[
            pltpu.VMEM((2, CHUNKS * NX * 8, 4 * stations), jnp.bfloat16),
            pltpu.VMEM((2 * CHUNKS * NX, 16, PIECE), jnp.bfloat16),
            pltpu.VMEM((CHUNKS, 2 * NX, 16, PIECE), jnp.bfloat16),
            pltpu.VMEM((2, 4 * SIDE, SIDE), jnp.float32),
            pltpu.VMEM((CHUNKS * PAIR * 2, 2, SIDE, SIDE), jnp.bfloat16),
            pltpu.SemaphoreType.DMA((CHUNKS,)),
            pltpu.SemaphoreType.DMA((CHUNKS,)),
            pltpu.SemaphoreType.DMA,
            pltpu.SemaphoreType.DMA,
            pltpu.SemaphoreType.DMA((CHUNKS + 1,)),
        ],
        compiler_params=pltpu.CompilerParams(
            collective_id=0, has_side_effects=True, vmem_limit_bytes=56 * 1024 * 1024
        ),
        name="beams",
    )(
        delay_table,
        dm_table,
        dm_index,
        bounds,
        jnp.asarray(cubes),
        delay_index.T,
        bounds,
        voltages.reshape(2, 2 * stations, HALF),
        jnp.asarray(dfts),
        jnp.asarray(planes),
    )

    rows = subbands // 2
    placed = pl.pallas_call(
        place_kernel,
        grid_spec=pltpu.PrefetchScalarGridSpec(
            num_scalar_prefetch=1,
            grid=(rows // BLOCK,),
            in_specs=[pl.BlockSpec((BLOCK, SIDE, SIDE), lambda i, bounds: (i, 0, 0))],
            out_specs=pl.BlockSpec((2, BLOCK, SIDE, SIDE), lambda i, bounds: (0, i, 0, 0)),
        ),
        out_shape=jax.ShapeDtypeStruct((2, rows, SIDE, SIDE), jnp.bfloat16),
        name="place",
    )(bounds, gathered.reshape(rows, SIDE, SIDE))
    placed = placed.reshape(subbands, SIDE // 2, 2, SIDE)
    return jnp.transpose(placed, (0, 2, 1, 3)).reshape(1, subbands, 2, HALF)


def solution(mesh):
    return jax.shard_map(
        per_device,
        mesh=mesh,
        in_specs=(P("sub", None, None, "section"), P(), P(), P(), P(), P()),
        out_specs=P("sub", None, None, "section"),
        check_vma=False,
    )
```

time: 170 us -> 137 us (0.81)
  local copies, waits for them, and re-layouts: 17.1 us -> 0 us
  other arithmetic: 14.2 us -> 0 us
  Pallas kernels: 138 us -> 135 us
    pallas_call x1, Pallas kernels: 138 us -> 127 us  [per_device(): pl.pallas_call(functools.partial(kernel, cosine_poly, sine_poly), out_sha...]
    select_n x1 -> x0, other arithmetic: 9.19 us -> none  [per_device(): placed = jnp.where(alive, rows, jnp.zeros((), jnp.bfloat16))]
    pallas_call x0 -> x1, Pallas kernels: none -> 8.49 us  [per_device(): pl.pallas_call(place_kernel, grid_spec=pltpu.PrefetchScalarGridSpec(num_s...]
    broadcast_in_dim x3 -> x0, local copies, waits for them, and re-layouts: 8.4 us -> none  [the longest x1 8.29 us: per_device(): placed = jnp.where(alive, rows, jnp.zeros((), jnp.bfloat16))]
    slice x3 -> x0, local copies, waits for them, and re-layouts: 2.6 us -> none  [the longest x2 2 us: in_chunk_order(): up = jnp.stack([turned[:, k, 0] for k in OFFSETS])]
    reshape x6 -> x0, local copies, waits for them, and re-layouts: 2.15 us -> none  [the longest x4 1.95 us: in_chunk_order(): grid = values.reshape((NX, NZ, 2, NY // 2) + values.shape[1:])]
    reduce_sum x2 -> x0, other arithmetic: 1.93 us -> none  [the longest x1 1.09 us: per_device(): delays = jnp.sum(jnp.where(picked, delay_table, 0.0), axis=-1)]
where the time goes in v2:
time: 137 us; the launch traced here: 135 us
  Pallas kernels  135 us (99%)
    pallas_call x1, Pallas kernels, per_device(): pl.pallas_call(functools.partial(kernel, cosine_poly, sine_poly), out_sha...  127 us
    pallas_call x1, Pallas kernels, per_device(): pl.pallas_call(place_kernel, grid_spec=pltpu.PrefetchScalarGridSpec(num_s...  8.49 us

profile of v2, /device:TPU:1, one launch (start us, length us, event | category | flops | bytes accessed | tf_op | source)
XLA Modules:
  0.0 135.4 jit_solution(11645684955786301035)
XLA Ops:
  0.0 126.9 %beams.1 = bf16[2,64,128,128]{3,2,1,0:T(8,128)(2,1)} custom-call(f32[64]{0:T(128)} %delay_table.1, f32[32]{0:T(128)} %dm_table.1, s32[128]{0:T(128)} %dm_index.1, s32[2,128]{1,0:T(2,128)} %bitcast.12, f32[256]{0:T(256)} %constant.6.clone.cubes, s32[48,128]{1,0:T(8,128)} %bitcast.11, s32[2,128]{1,0:T(2,128)} %bitcast.13, bf16[2,96,8192]{2,1,0:T(8,128)(2,1)} %bitcast.10, ...), custom_call_target="tpu_custom_call" | custom-call | tf_op jit(solution)/shard_map/beams/pallas_call | solution.py:419
  126.9 8.5 %place.1 = bf16[2,128,128,128]{3,2,1,0:T(8,128)(2,1)} custom-call(s32[2,128]{1,0:T(2,128)} %bitcast.14, bf16[128,128,128]{2,1,0:T(8,128)(2,1)} %bitcast.9), custom_call_target="tpu_custom_call" | custom-call | tf_op jit(solution)/shard_map/place/pallas_call | solution.py:454

commit v3 on v2

--- a/solution.py
+++ b/solution.py
@@ -18,7 +18,7 @@
 PIECE = HALF // PIECES
 PAIR = 2
 CHUNKS = NZ * NY // PAIR
-AHEAD = 3
+AHEAD = 2
 LANES = 256
 
 
@@ -101,10 +101,13 @@
     cubes,
     delay_index,
     bounds,
+    voltages_far,
+    dfts_far,
+    planes_far,
+    gathered,
     voltages,
     dfts,
     planes,
-    gathered,
     weights,
     formed,
     arrived,
@@ -115,7 +118,17 @@
     z_send,
     z_recv,
     own_sem,
+    load_sem,
 ):
+    loads = [
+        pltpu.make_async_copy(far, near, load_sem.at[index])
+        for index, (far, near) in enumerate(
+            [(voltages_far, voltages), (dfts_far, dfts), (planes_far, planes)]
+        )
+    ]
+    for load in loads:
+        load.start()
+
     me = lax.axis_index("sub")
     core = lax.axis_index("section")
     my_x = me // (NZ * NY)
@@ -161,14 +174,17 @@
         0, delay_table.shape[0], look_up, jnp.zeros((stations, beams), jnp.float32), unroll=8
     )
     row = lax.broadcasted_iota(jnp.int32, (CHUNKS * NX * 8, 1), 0)
-    row_chunk = row // (NX * 8)
-    row_pair = (row // 2) % PAIR
-    row_z = (my_z + (1 - 2 * row_pair) * chunk_offset(row_chunk) + NZ) % NZ
-    row_beam = ((row // 8) % NX) * (NZ * NY) + row_z * NY + PAIR * row_pair + row_chunk % 2
+    row_chunk = row >> 5
+    row_index = row_chunk >> 1
+    row_offset = NZ // 2 + ((row_index + 1) >> 1) * (1 - 2 * (row_index & 1))
+    row_pair = (row >> 1) & 1
+    row_z = (my_z + (1 - 2 * row_pair) * row_offset + 2 * NZ) & (NZ - 1)
+    row_beam = ((row >> 3) & (NX - 1)) * (NZ * NY) + row_z * NY + PAIR * row_pair + (row_chunk & 1)
     column = lax.broadcasted_iota(jnp.int32, (CHUNKS * NX * 8, 2 * beams), 1)
-    chosen = jnp.where(column == (row % 2) * beams + row_beam, 1.0, 0.0).astype(jnp.bfloat16)
-    piece_of_row = (row // 4) % 2
-    piece_of_lane = lax.broadcasted_iota(jnp.int32, (CHUNKS * NX * 8, 4 * stations), 1) // (2 * stations)
+    chosen = jnp.where(column == (row & 1) * beams + row_beam, 1.0, 0.0).astype(jnp.bfloat16)
+    piece_of_row = (row >> 2) & 1
+    lane = lax.broadcasted_iota(jnp.int32, (CHUNKS * NX * 8, 4 * stations), 1)
+    piece_of_lane = jnp.where(lane >= 2 * stations, 1, 0)
     scaling = 1.0 / math.sqrt(stations)
     for local in range(2):
         subband = 2 * me + local
@@ -192,7 +208,7 @@
 
     tiles = PIECE // LANES
 
-    def form(step, carry):
+    def form(first, count, step, carry):
         local = step // tiles
         start = lax.rem(step, tiles) * LANES
         parts = []
@@ -203,15 +219,21 @@
                 ]
                 for piece in range(2)
             ]
-            product = dot(weights[local], jnp.concatenate(blocks, axis=0))
-            parts.append(product.reshape(CHUNKS * NX, 8, LANES))
+            product = dot(
+                weights[local, first * NX * 8 : (first + count) * NX * 8],
+                jnp.concatenate(blocks, axis=0),
+            )
+            parts.append(product.reshape(count * NX, 8, LANES))
         both = jnp.concatenate(parts, axis=1).astype(jnp.bfloat16)
         formed[
-            pl.ds(local * (CHUNKS * NX), CHUNKS * NX), :, pl.ds(pl.multiple_of(start, LANES), LANES)
+            pl.ds(local * (CHUNKS * NX) + first * NX, count * NX),
+            :,
+            pl.ds(pl.multiple_of(start, LANES), LANES),
         ] = both
         return carry
 
-    lax.fori_loop(0, 2 * tiles, form, 0)
+    loads[0].wait()
+    lax.fori_loop(0, 2 * tiles, functools.partial(form, 0, 1), 0)
 
     pl.semaphore_wait(barrier, 2 * NX - 2 + 2 * NZ * NY - 1)
 
@@ -244,8 +266,12 @@
             formed.at[pl.ds(0, 2 * NX - 1)], formed.at[pl.ds(0, 2 * NX - 1)], x_send.at[chunk]
         ).wait()
 
-    for chunk in range(AHEAD):
-        start_x(chunk)
+    start_x(0)
+    lax.fori_loop(0, 2 * tiles, functools.partial(form, 1, CHUNKS - 1), 0)
+    for load in loads[1:]:
+        load.wait()
+    wait_x_sent(0)
+    start_x(1)
 
     slot = (my_z * NY + my_y) * 2 + core
 
@@ -379,7 +405,7 @@
 
     lax.fori_loop(0, CHUNKS, do_chunk, 0)
 
-    for chunk in range(CHUNKS):
+    for chunk in range(1, CHUNKS):
         wait_x_sent(chunk)
     others = 2 * NZ * NY - 1
     pltpu.make_async_copy(
@@ -391,19 +417,78 @@
     ).wait()
 
 
-BLOCK = 16
-
-
-def place_kernel(bounds, gathered, placed):
+BLOCK = 8
+PARTS = 4
+
+
+def place_kernel(bounds, gathered, placed, rows, blank, in_sem, out_sem):
     me = lax.axis_index("sub")
     start, end = bounds[0, me], bounds[1, me]
-    rows = placed.shape[1] * pl.num_programs(0)
-    first = pl.program_id(0) * BLOCK
-    for high in range(2):
-        row = high * rows + first + lax.broadcasted_iota(jnp.int32, (BLOCK, 1, 1), 0)
-        live = jnp.logical_and(row >= start, row < end)
-        value = jnp.where(live, gathered[...].astype(jnp.float32), 0.0)
-        placed[high] = value.astype(jnp.bfloat16)
+    count = gathered.shape[0]
+    part = count // PARTS
+    loads = [
+        pltpu.make_async_copy(
+            gathered.at[pl.ds(p * part, part)], rows.at[pl.ds(p * part, part)], in_sem.at[p]
+        )
+        for p in range(PARTS)
+    ]
+    for load in loads:
+        load.start()
+    blank[...] = jnp.zeros_like(blank)
+
+    def write_blank(block, carry):
+        first = block * BLOCK
+
+        @pl.when(jnp.logical_or(first + BLOCK <= start, first >= end))
+        def _():
+            pltpu.make_async_copy(blank, placed.at[pl.ds(first, BLOCK)], out_sem).start()
+
+        return carry
+
+    lax.fori_loop(0, 2 * count // BLOCK, write_blank, 0)
+
+    def write_rows(block, carry):
+        source = block * BLOCK
+        for high in range(2):
+            first = source + high * count
+            whole = jnp.logical_and(first >= start, first + BLOCK <= end)
+            some = jnp.logical_and(first < end, first + BLOCK > start)
+
+            @pl.when(whole)
+            def _():
+                pltpu.make_async_copy(
+                    rows.at[pl.ds(source, BLOCK)], placed.at[pl.ds(first, BLOCK)], out_sem
+                ).start()
+
+            @pl.when(jnp.logical_and(some, jnp.logical_not(whole)))
+            def _():
+                def one(index, carry):
+                    row = first + index
+                    live = jnp.logical_and(row >= start, row < end)
+
+                    @pl.when(live)
+                    def _():
+                        pltpu.make_async_copy(
+                            rows.at[pl.ds(source + index, 1)], placed.at[pl.ds(row, 1)], out_sem
+                        ).start()
+
+                    @pl.when(jnp.logical_not(live))
+                    def _():
+                        pltpu.make_async_copy(
+                            blank.at[pl.ds(0, 1)], placed.at[pl.ds(row, 1)], out_sem
+                        ).start()
+
+                    return carry
+
+                lax.fori_loop(0, BLOCK, one, 0)
+
+        return carry
+
+    blocks = part // BLOCK
+    for p in range(PARTS):
+        loads[p].wait()
+        lax.fori_loop(p * blocks, (p + 1) * blocks, write_rows, 0)
+    pltpu.make_async_copy(placed, placed, out_sem).wait()
 
 
 def per_device(voltages, delay_table, delay_index, dm_table, dm_index, range_bounds):
@@ -415,13 +500,17 @@
     cosine_poly, sine_poly = turn_coefficients()
     vmem = pl.BlockSpec(memory_space=pltpu.VMEM)
     smem = pl.BlockSpec(memory_space=pltpu.SMEM)
+    far = pl.BlockSpec(memory_space=pl.ANY)
     bounds = range_bounds.T
     gathered = pl.pallas_call(
         functools.partial(kernel, cosine_poly, sine_poly),
         out_shape=jax.ShapeDtypeStruct((2, NZ * NY * 2, SIDE, SIDE), jnp.bfloat16),
-        in_specs=[smem] * 5 + [vmem] * 5,
-        out_specs=pl.BlockSpec(memory_space=pl.ANY),
+        in_specs=[smem] * 5 + [vmem] * 2 + [far] * 3,
+        out_specs=far,
         scratch_shapes=[
+            pltpu.VMEM((2, 2 * stations, HALF), jnp.bfloat16),
+            pltpu.VMEM(dfts.shape, dfts.dtype),
+            pltpu.VMEM(planes.shape, planes.dtype),
             pltpu.VMEM((2, CHUNKS * NX * 8, 4 * stations), jnp.bfloat16),
             pltpu.VMEM((2 * CHUNKS * NX, 16, PIECE), jnp.bfloat16),
             pltpu.VMEM((CHUNKS, 2 * NX, 16, PIECE), jnp.bfloat16),
@@ -432,6 +521,7 @@
             pltpu.SemaphoreType.DMA,
             pltpu.SemaphoreType.DMA,
             pltpu.SemaphoreType.DMA((CHUNKS + 1,)),
+            pltpu.SemaphoreType.DMA((3,)),
         ],
         compiler_params=pltpu.CompilerParams(
             collective_id=0, has_side_effects=True, vmem_limit_bytes=56 * 1024 * 1024
@@ -453,13 +543,16 @@
     rows = subbands // 2
     placed = pl.pallas_call(
         place_kernel,
-        grid_spec=pltpu.PrefetchScalarGridSpec(
-            num_scalar_prefetch=1,
-            grid=(rows // BLOCK,),
-            in_specs=[pl.BlockSpec((BLOCK, SIDE, SIDE), lambda i, bounds: (i, 0, 0))],
-            out_specs=pl.BlockSpec((2, BLOCK, SIDE, SIDE), lambda i, bounds: (0, i, 0, 0)),
-        ),
-        out_shape=jax.ShapeDtypeStruct((2, rows, SIDE, SIDE), jnp.bfloat16),
+        in_specs=[smem, far],
+        out_specs=far,
+        out_shape=jax.ShapeDtypeStruct((subbands, SIDE, SIDE), jnp.bfloat16),
+        scratch_shapes=[
+            pltpu.VMEM((rows, SIDE, SIDE), jnp.bfloat16),
+            pltpu.VMEM((BLOCK, SIDE, SIDE), jnp.bfloat16),
+            pltpu.SemaphoreType.DMA((PARTS,)),
+            pltpu.SemaphoreType.DMA,
+        ],
+        compiler_params=pltpu.CompilerParams(vmem_limit_bytes=56 * 1024 * 1024),
         name="place",
     )(bounds, gathered.reshape(rows, SIDE, SIDE))
     placed = placed.reshape(subbands, SIDE // 2, 2, SIDE)

time: 137 us -> 131 us (0.956)
  Pallas kernels: 135 us -> 129 us
    pallas_call x1, Pallas kernels: 127 us -> 124 us  [per_device(): pl.pallas_call(functools.partial(kernel, cosine_poly, sine_poly), out_sha...]
    pallas_call x1, Pallas kernels: 8.49 us -> 5.71 us  [per_device(): pl.pallas_call(place_kernel, in_specs=[smem, far], out_specs=far, out_sha...]
where the time goes in v3:
time: 131 us; the launch traced here: 129 us
  Pallas kernels  129 us (98%)
    pallas_call x1, Pallas kernels, per_device(): pl.pallas_call(functools.partial(kernel, cosine_poly, sine_poly), out_sha...  124 us
    pallas_call x1, Pallas kernels, per_device(): pl.pallas_call(place_kernel, in_specs=[smem, far], out_specs=far, out_sha...  5.71 us

profile of v3, /device:TPU:1, one launch (start us, length us, event | category | flops | bytes accessed | tf_op | source)
XLA Modules:
  0.0 129.3 jit_solution(2155934303117823138)
XLA Ops:
  0.0 123.6 %beams.1 = bf16[2,64,128,128]{3,2,1,0:T(8,128)(2,1)} custom-call(f32[64]{0:T(128)} %delay_table.1, f32[32]{0:T(128)} %dm_table.1, s32[128]{0:T(128)} %dm_index.1, s32[2,128]{1,0:T(2,128)} %bitcast.12, f32[256]{0:T(256)} %constant.6.clone.cubes, s32[48,128]{1,0:T(8,128)} %bitcast.11, s32[2,128]{1,0:T(2,128)} %bitcast.13, bf16[2,96,8192]{2,1,0:T(8,128)(2,1)} %bitcast.10, ...), custom_call_target="tpu_custom_call" | custom-call | tf_op jit(solution)/shard_map/beams/pallas_call | solution.py:505
  123.6 5.7 %place.1 = bf16[256,128,128]{2,1,0:T(8,128)(2,1)} custom-call(s32[2,128]{1,0:T(2,128)} %bitcast.14, bf16[128,128,128]{2,1,0:T(8,128)(2,1)} %bitcast.9), custom_call_target="tpu_custom_call" | custom-call | tf_op jit(solution)/shard_map/place/pallas_call | solution.py:544

commit v4 on v3

--- a/solution.py
+++ b/solution.py
@@ -173,19 +173,8 @@
     delays = lax.fori_loop(
         0, delay_table.shape[0], look_up, jnp.zeros((stations, beams), jnp.float32), unroll=8
     )
-    row = lax.broadcasted_iota(jnp.int32, (CHUNKS * NX * 8, 1), 0)
-    row_chunk = row >> 5
-    row_index = row_chunk >> 1
-    row_offset = NZ // 2 + ((row_index + 1) >> 1) * (1 - 2 * (row_index & 1))
-    row_pair = (row >> 1) & 1
-    row_z = (my_z + (1 - 2 * row_pair) * row_offset + 2 * NZ) & (NZ - 1)
-    row_beam = ((row >> 3) & (NX - 1)) * (NZ * NY) + row_z * NY + PAIR * row_pair + (row_chunk & 1)
-    column = lax.broadcasted_iota(jnp.int32, (CHUNKS * NX * 8, 2 * beams), 1)
-    chosen = jnp.where(column == (row & 1) * beams + row_beam, 1.0, 0.0).astype(jnp.bfloat16)
-    piece_of_row = (row >> 2) & 1
-    lane = lax.broadcasted_iota(jnp.int32, (CHUNKS * NX * 8, 4 * stations), 1)
-    piece_of_lane = jnp.where(lane >= 2 * stations, 1, 0)
     scaling = 1.0 / math.sqrt(stations)
+    sources = []
     for local in range(2):
         subband = 2 * me + local
         freq = 1.0 + (subband.astype(jnp.float32) + 0.5) * (1.0 / subbands)
@@ -200,12 +189,31 @@
             ],
             axis=0,
         )
-        source = jnp.concatenate([both, both], axis=0).astype(jnp.bfloat16)
-        placed = lax.dot_general(
-            chosen, source, (((1,), (1,)), ((), ())), preferred_element_type=jnp.float32
-        )
-        weights[local] = jnp.where(piece_of_row == piece_of_lane, placed, 0.0).astype(jnp.bfloat16)
-
+        sources.append(jnp.concatenate([both, both], axis=0).astype(jnp.bfloat16))
+
+    def weigh(first, count):
+        height = count * NX * 8
+        row = first * NX * 8 + lax.broadcasted_iota(jnp.int32, (height, 1), 0)
+        row_chunk = row >> 5
+        row_index = row_chunk >> 1
+        row_offset = NZ // 2 + ((row_index + 1) >> 1) * (1 - 2 * (row_index & 1))
+        row_pair = (row >> 1) & 1
+        row_z = (my_z + (1 - 2 * row_pair) * row_offset + 2 * NZ) & (NZ - 1)
+        row_y = (my_y + PAIR * row_pair + (row_chunk & 1)) & (NY - 1)
+        row_beam = ((row >> 3) & (NX - 1)) * (NZ * NY) + row_z * NY + row_y
+        column = lax.broadcasted_iota(jnp.int32, (height, 2 * beams), 1)
+        chosen = jnp.where(column == (row & 1) * beams + row_beam, 1.0, 0.0).astype(jnp.bfloat16)
+        lane = lax.broadcasted_iota(jnp.int32, (height, 4 * stations), 1)
+        same = ((row >> 2) & 1) == jnp.where(lane >= 2 * stations, 1, 0)
+        for local in range(2):
+            placed = lax.dot_general(
+                chosen, sources[local], (((1,), (1,)), ((), ())), preferred_element_type=jnp.float32
+            )
+            weights[local, first * NX * 8 : (first + count) * NX * 8] = jnp.where(
+                same, placed, 0.0
+            ).astype(jnp.bfloat16)
+
+    weigh(0, 1)
     tiles = PIECE // LANES
 
     def form(first, count, step, carry):
@@ -239,11 +247,13 @@
 
     def x_copy(chunk, step):
         other_x, other_core = x_partner(step)
+        group = lax.rem(step // 2, 2)
+        place = group * NX + (step // NX) * 2 + lax.rem(step, 2)
         return pltpu.make_async_remote_copy(
             src_ref=formed.at[(other_core * CHUNKS + chunk) * NX + other_x],
-            dst_ref=arrived.at[chunk, step],
+            dst_ref=arrived.at[chunk, place],
             send_sem=x_send.at[chunk],
-            recv_sem=x_recv.at[chunk],
+            recv_sem=x_recv.at[chunk * 2 + group],
             device_id=((other_x * NZ + my_z) * NY + my_y, other_core),
             device_id_type=MESH,
         )
@@ -258,8 +268,11 @@
             x_copy(chunk, step).start()
             return carry
 
-        lax.fori_loop(1, 2 * NX, one, 0)
+        lax.fori_loop(NX, NX + 2, one, 0)
+        x_copy(chunk, 1).start()
         own_copy(chunk).start()
+        lax.fori_loop(2, NX, one, 0)
+        lax.fori_loop(NX + 2, 2 * NX, one, 0)
 
     def wait_x_sent(chunk):
         pltpu.make_async_copy(
@@ -267,6 +280,7 @@
         ).wait()
 
     start_x(0)
+    weigh(1, CHUNKS - 1)
     lax.fori_loop(0, 2 * tiles, functools.partial(form, 1, CHUNKS - 1), 0)
     for load in loads[1:]:
         load.wait()
@@ -275,135 +289,138 @@
 
     slot = (my_z * NY + my_y) * 2 + core
 
-    def do_chunk(chunk, carry):
-        pltpu.make_async_copy(
-            arrived.at[chunk, pl.ds(1, 2 * NX - 1)],
-            arrived.at[chunk, pl.ds(1, 2 * NX - 1)],
-            x_recv.at[chunk],
-        ).wait()
-        own_copy(chunk).wait()
-
-        @pl.when(chunk < CHUNKS - AHEAD)
+    def do_half(step, carry):
+        chunk = step // 2
+        group = lax.rem(step, 2)
+
+        @pl.when(group == 0)
         def _():
-            start_x(chunk + AHEAD)
+            near = arrived.at[chunk, pl.ds(1, NX - 1)]
+            pltpu.make_async_copy(near, near, x_recv.at[step]).wait()
+            own_copy(chunk).wait()
+
+            @pl.when(chunk < CHUNKS - AHEAD)
+            def _():
+                start_x(chunk + AHEAD)
+
+        @pl.when(group == 1)
+        def _():
+            far = arrived.at[chunk, pl.ds(NX, NX)]
+            pltpu.make_async_copy(far, far, x_recv.at[step]).wait()
 
         offset = chunk_offset(chunk)
-
-        def fold(step, carry):
-            group = step // 2
-            other = lax.rem(step, 2)
+        parity = lax.rem(my_x + group, 2)
+
+        def fold(other, carry):
             half = lax.rem(core + other, 2)
 
             def lane_tile(index, carry):
                 lanes = pl.ds(pl.multiple_of(index * SIDE, SIDE), SIDE)
-                near = arrived[chunk, group * 2 + other, :, lanes].astype(jnp.float32)
-                far = arrived[chunk, group * 2 + 4 + other, :, lanes].astype(jnp.float32)
+                near = arrived[chunk, group * NX + other, :, lanes].astype(jnp.float32)
+                far = arrived[chunk, group * NX + 2 + other, :, lanes].astype(jnp.float32)
                 total = near + far
                 row = half * (SIDE // 4) + index
-                grid[group, pl.ds(row, 8, stride=SIDE // 2), :] = total[:8]
-                grid[group, pl.ds(row + SIDE // 8, 8, stride=SIDE // 2), :] = total[8:]
+                grid[pl.ds(row, 8, stride=SIDE // 2), :] = total[:8]
+                grid[pl.ds(row + SIDE // 8, 8, stride=SIDE // 2), :] = total[8:]
                 return carry
 
             lax.fori_loop(0, PIECE // SIDE, lane_tile, 0, unroll=4)
             return carry
 
-        lax.fori_loop(0, 4, fold, 0)
-
-        def transform(beam, carry):
+        lax.fori_loop(0, 2, fold, 0)
+
+        def target_beam(beam):
             other_z = lax.rem(my_z + (1 - 2 * beam) * offset + NZ, NZ)
-            other_y = PAIR * beam + lax.rem(chunk, 2)
-            beam_id = plane_start + other_z * NY + other_y
+            other_y = lax.rem(my_y + PAIR * beam + lax.rem(chunk, 2), NY)
+            return plane_start + other_z * NY + other_y
+
+        series = []
+        for beam in range(PAIR):
+            pieces = [
+                grid[pl.ds((piece * 4 + beam * 2 + part) * (SIDE // 2), SIDE // 2), :]
+                for part in range(2)
+                for piece in range(2)
+            ]
+            series.append(jnp.concatenate(pieces, axis=0))
+        series = jnp.concatenate(series, axis=1).astype(jnp.bfloat16)
+        low_row = parity * (subbands // 4) + 2 * (my_z * NY + my_y) + core
+        high_row = low_row + subbands // 2
+        stage = dot(dfts[0, 0], series) + dot(dfts[0, 1], series)
+        cosine, sine = planes[0], planes[1]
+        turned = []
+        for beam in range(PAIR):
+            lanes = slice(beam * SIDE, (beam + 1) * SIDE)
+            real, imag = stage[:SIDE, lanes], stage[SIDE:, lanes]
+            turned.append(
+                jnp.concatenate([real * cosine + imag * sine, imag * cosine - real * sine], axis=1)
+            )
+        high, low = split(jnp.concatenate(turned, axis=0))
+        stage = dot(high, dfts[1, 0]) + dot(high, dfts[1, 1]) + dot(low, dfts[1, 0])
+        turned = []
+        for beam in range(PAIR):
+            rows_of = slice(beam * SIDE, (beam + 1) * SIDE)
+            real, imag = stage[rows_of, :SIDE], stage[rows_of, SIDE:]
+            beam_id = target_beam(beam)
+            is_high = jnp.logical_and(
+                bounds_scalar[0, beam_id] <= high_row, bounds_scalar[1, beam_id] > high_row
+            )
             strength = dm_table[dm_index[beam_id]]
-            series = []
-            for group in range(2):
-                pieces = [
-                    grid[
-                        group,
-                        pl.ds(pl.multiple_of((piece * 4 + beam * 2) * (SIDE // 2) + part * (SIDE // 2), SIDE // 2), SIDE // 2),
-                        :,
-                    ]
-                    for part in range(2)
-                    for piece in range(2)
-                ]
-                series.append(jnp.concatenate(pieces, axis=0))
-            series = jnp.concatenate(series, axis=1).astype(jnp.bfloat16)
-            stage = dot(dfts[0, 0], series) + dot(dfts[0, 1], series)
-            cosine, sine = planes[0], planes[1]
-            turned = []
-            for group in range(2):
-                lanes = slice(group * SIDE, (group + 1) * SIDE)
-                real, imag = stage[:SIDE, lanes], stage[SIDE:, lanes]
-                turned.append(
-                    jnp.concatenate([real * cosine + imag * sine, imag * cosine - real * sine], axis=1)
+            dispersion = strength * cubes[jnp.where(is_high, high_row, low_row)]
+            chirp_cos, chirp_sin = turn_cos_sin(dispersion * planes[2], cosine_poly, sine_poly)
+            turned.append(
+                jnp.concatenate(
+                    [real * chirp_cos - imag * chirp_sin, real * chirp_sin + imag * chirp_cos], axis=1
                 )
-            high, low = split(jnp.concatenate(turned, axis=0))
-            stage = dot(high, dfts[1, 0]) + dot(high, dfts[1, 1]) + dot(low, dfts[1, 0])
-            turned = []
-            for group in range(2):
-                rows_of = slice(group * SIDE, (group + 1) * SIDE)
-                real, imag = stage[rows_of, :SIDE], stage[rows_of, SIDE:]
-                low_row = lax.rem(my_x + group, 2) * (subbands // 4) + 2 * (my_z * NY + my_y) + core
-                high_row = low_row + subbands // 2
-                is_high = jnp.logical_and(
-                    bounds_scalar[0, beam_id] <= high_row, bounds_scalar[1, beam_id] > high_row
-                )
-                dispersion = strength * cubes[jnp.where(is_high, high_row, low_row)]
-                chirp_cos, chirp_sin = turn_cos_sin(dispersion * planes[2], cosine_poly, sine_poly)
-                turned.append(
-                    jnp.concatenate(
-                        [real * chirp_cos - imag * chirp_sin, real * chirp_sin + imag * chirp_cos], axis=1
-                    )
-                )
-            high, low = split(jnp.concatenate(turned, axis=0))
-            stage = dot(high, dfts[2, 0]) + dot(high, dfts[2, 1]) + dot(low, dfts[2, 0])
-            turned = []
-            for group in range(2):
-                rows_of = slice(group * SIDE, (group + 1) * SIDE)
-                real, imag = stage[rows_of, :SIDE], stage[rows_of, SIDE:]
-                turned.append(
-                    jnp.concatenate([real * cosine - imag * sine, real * sine + imag * cosine], axis=0)
-                )
-            high, low = split(jnp.concatenate(turned, axis=1))
-            final = dot(dfts[3, 0], high) + dot(dfts[3, 1], high) + dot(dfts[3, 0], low)
-            final = final.astype(jnp.bfloat16)
+            )
+        high, low = split(jnp.concatenate(turned, axis=0))
+        stage = dot(high, dfts[2, 0]) + dot(high, dfts[2, 1]) + dot(low, dfts[2, 0])
+        turned = []
+        for beam in range(PAIR):
+            rows_of = slice(beam * SIDE, (beam + 1) * SIDE)
+            real, imag = stage[rows_of, :SIDE], stage[rows_of, SIDE:]
+            turned.append(
+                jnp.concatenate([real * cosine - imag * sine, real * sine + imag * cosine], axis=0)
+            )
+        high, low = split(jnp.concatenate(turned, axis=1))
+        final = dot(dfts[3, 0], high) + dot(dfts[3, 1], high) + dot(dfts[3, 0], low)
+        final = final.astype(jnp.bfloat16)
+        for beam in range(PAIR):
             for section in range(2):
                 message = (chunk * PAIR + beam) * 2 + section
-                for group in range(2):
-                    parity = lax.rem(my_x + group, 2)
-                    results[message, parity] = final[
-                        section * SIDE : (section + 1) * SIDE, group * SIDE : (group + 1) * SIDE
-                    ]
-
-            def send(section, carry):
-                message = (chunk * PAIR + beam) * 2 + section
-                own = jnp.logical_and(beam_id == me, section == core)
-
-                @pl.when(own)
-                def _():
-                    pltpu.make_async_copy(
-                        results.at[message], gathered.at[:, slot], own_sem.at[CHUNKS]
-                    ).start()
-
-                @pl.when(jnp.logical_not(own))
-                def _():
-                    pltpu.make_async_remote_copy(
-                        src_ref=results.at[message],
-                        dst_ref=gathered.at[:, slot],
-                        send_sem=z_send,
-                        recv_sem=z_recv,
-                        device_id=(beam_id, section),
-                        device_id_type=MESH,
-                    ).start()
-
-                return carry
-
-            lax.fori_loop(0, 2, send, 0)
+                results[message, parity] = final[
+                    section * SIDE : (section + 1) * SIDE, beam * SIDE : (beam + 1) * SIDE
+                ]
+
+        def send(index, carry):
+            beam = index // 2
+            section = lax.rem(index, 2)
+            beam_id = target_beam(beam)
+            message = chunk * (2 * PAIR) + index
+            own = jnp.logical_and(beam_id == me, section == core)
+
+            @pl.when(own)
+            def _():
+                pltpu.make_async_copy(
+                    results.at[message, parity], gathered.at[parity, slot], own_sem.at[CHUNKS]
+                ).start()
+
+            @pl.when(jnp.logical_not(own))
+            def _():
+                pltpu.make_async_remote_copy(
+                    src_ref=results.at[message, parity],
+                    dst_ref=gathered.at[parity, slot],
+                    send_sem=z_send,
+                    recv_sem=z_recv,
+                    device_id=(beam_id, section),
+                    device_id_type=MESH,
+                ).start()
+
             return carry
 
-        lax.fori_loop(0, PAIR, transform, 0)
+        lax.fori_loop(0, 2 * PAIR, send, 0)
         return carry
 
-    lax.fori_loop(0, CHUNKS, do_chunk, 0)
+    lax.fori_loop(0, 2 * CHUNKS, do_half, 0)
 
     for chunk in range(1, CHUNKS):
         wait_x_sent(chunk)
@@ -514,10 +531,10 @@
             pltpu.VMEM((2, CHUNKS * NX * 8, 4 * stations), jnp.bfloat16),
             pltpu.VMEM((2 * CHUNKS * NX, 16, PIECE), jnp.bfloat16),
             pltpu.VMEM((CHUNKS, 2 * NX, 16, PIECE), jnp.bfloat16),
-            pltpu.VMEM((2, 4 * SIDE, SIDE), jnp.float32),
+            pltpu.VMEM((4 * SIDE, SIDE), jnp.float32),
             pltpu.VMEM((CHUNKS * PAIR * 2, 2, SIDE, SIDE), jnp.bfloat16),
             pltpu.SemaphoreType.DMA((CHUNKS,)),
-            pltpu.SemaphoreType.DMA((CHUNKS,)),
+            pltpu.SemaphoreType.DMA((2 * CHUNKS,)),
             pltpu.SemaphoreType.DMA,
             pltpu.SemaphoreType.DMA,
             pltpu.SemaphoreType.DMA((CHUNKS + 1,)),

time: 131 us -> 127 us (0.969)
  Pallas kernels: 129 us -> 126 us
    pallas_call x1, Pallas kernels: 124 us -> 120 us  [per_device(): pl.pallas_call(functools.partial(kernel, cosine_poly, sine_poly), out_sha...]
where the time goes in v4:
time: 127 us; the launch traced here: 126 us
  Pallas kernels  126 us (99%)
    pallas_call x1, Pallas kernels, per_device(): pl.pallas_call(functools.partial(kernel, cosine_poly, sine_poly), out_sha...  120 us
    pallas_call x1, Pallas kernels, per_device(): pl.pallas_call(place_kernel, in_specs=[smem, far], out_specs=far, out_sha...  6.32 us

profile of v4, /device:TPU:1, one launch (start us, length us, event | category | flops | bytes accessed | tf_op | source)
XLA Modules:
  0.0 126.1 jit_solution(9419032817980016677)
XLA Ops:
  0.0 119.8 %beams.1 = bf16[2,64,128,128]{3,2,1,0:T(8,128)(2,1)} custom-call(f32[64]{0:T(128)} %delay_table.1, f32[32]{0:T(128)} %dm_table.1, s32[128]{0:T(128)} %dm_index.1, s32[2,128]{1,0:T(2,128)} %bitcast.12, f32[256]{0:T(256)} %constant.6.clone.cubes, s32[48,128]{1,0:T(8,128)} %bitcast.11, s32[2,128]{1,0:T(2,128)} %bitcast.13, bf16[2,96,8192]{2,1,0:T(8,128)(2,1)} %bitcast.10, ...), custom_call_target="tpu_custom_call" | custom-call | tf_op jit(solution)/shard_map/beams/pallas_call | solution.py:522
  119.8 6.3 %place.1 = bf16[256,128,128]{2,1,0:T(8,128)(2,1)} custom-call(s32[2,128]{1,0:T(2,128)} %bitcast.14, bf16[128,128,128]{2,1,0:T(8,128)(2,1)} %bitcast.9), custom_call_target="tpu_custom_call" | custom-call | tf_op jit(solution)/shard_map/place/pallas_call | solution.py:561

commit v5 on v4

--- a/solution.py
+++ b/solution.py
@@ -158,8 +158,8 @@
         )
         return carry
 
-    lax.fori_loop(2, 2 * NX, greet_x, 0)
-    lax.fori_loop(1, 2 * NZ * NY, greet_plane, 0)
+    lax.fori_loop(2, 2 * NX, greet_x, 0, unroll=True)
+    lax.fori_loop(1, 2 * NZ * NY, greet_plane, 0, unroll=9)
 
     beams = NX * NZ * NY
     stations = delay_index.shape[0]
@@ -435,22 +435,12 @@
 
 
 BLOCK = 8
-PARTS = 4
-
-
-def place_kernel(bounds, gathered, placed, rows, blank, in_sem, out_sem):
+
+
+def place_kernel(bounds, gathered, placed, blank, out_sem):
     me = lax.axis_index("sub")
     start, end = bounds[0, me], bounds[1, me]
     count = gathered.shape[0]
-    part = count // PARTS
-    loads = [
-        pltpu.make_async_copy(
-            gathered.at[pl.ds(p * part, part)], rows.at[pl.ds(p * part, part)], in_sem.at[p]
-        )
-        for p in range(PARTS)
-    ]
-    for load in loads:
-        load.start()
     blank[...] = jnp.zeros_like(blank)
 
     def write_blank(block, carry):
@@ -474,7 +464,7 @@
             @pl.when(whole)
             def _():
                 pltpu.make_async_copy(
-                    rows.at[pl.ds(source, BLOCK)], placed.at[pl.ds(first, BLOCK)], out_sem
+                    gathered.at[pl.ds(source, BLOCK)], placed.at[pl.ds(first, BLOCK)], out_sem
                 ).start()
 
             @pl.when(jnp.logical_and(some, jnp.logical_not(whole)))
@@ -486,7 +476,7 @@
                     @pl.when(live)
                     def _():
                         pltpu.make_async_copy(
-                            rows.at[pl.ds(source + index, 1)], placed.at[pl.ds(row, 1)], out_sem
+                            gathered.at[pl.ds(source + index, 1)], placed.at[pl.ds(row, 1)], out_sem
                         ).start()
 
                     @pl.when(jnp.logical_not(live))
@@ -501,10 +491,7 @@
 
         return carry
 
-    blocks = part // BLOCK
-    for p in range(PARTS):
-        loads[p].wait()
-        lax.fori_loop(p * blocks, (p + 1) * blocks, write_rows, 0)
+    lax.fori_loop(0, count // BLOCK, write_rows, 0)
     pltpu.make_async_copy(placed, placed, out_sem).wait()
 
 
@@ -521,7 +508,7 @@
     bounds = range_bounds.T
     gathered = pl.pallas_call(
         functools.partial(kernel, cosine_poly, sine_poly),
-        out_shape=jax.ShapeDtypeStruct((2, NZ * NY * 2, SIDE, SIDE), jnp.bfloat16),
+        out_shape=pltpu.VMEM((2, NZ * NY * 2, SIDE, SIDE), jnp.bfloat16),
         in_specs=[smem] * 5 + [vmem] * 2 + [far] * 3,
         out_specs=far,
         scratch_shapes=[
@@ -541,7 +528,7 @@
             pltpu.SemaphoreType.DMA((3,)),
         ],
         compiler_params=pltpu.CompilerParams(
-            collective_id=0, has_side_effects=True, vmem_limit_bytes=56 * 1024 * 1024
+            collective_id=0, has_side_effects=True, vmem_limit_bytes=54 * 1024 * 1024
         ),
         name="beams",
     )(
@@ -564,12 +551,10 @@
         out_specs=far,
         out_shape=jax.ShapeDtypeStruct((subbands, SIDE, SIDE), jnp.bfloat16),
         scratch_shapes=[
-            pltpu.VMEM((rows, SIDE, SIDE), jnp.bfloat16),
             pltpu.VMEM((BLOCK, SIDE, SIDE), jnp.bfloat16),
-            pltpu.SemaphoreType.DMA((PARTS,)),
             pltpu.SemaphoreType.DMA,
         ],
-        compiler_params=pltpu.CompilerParams(vmem_limit_bytes=56 * 1024 * 1024),
+        compiler_params=pltpu.CompilerParams(vmem_limit_bytes=16 * 1024 * 1024),
         name="place",
     )(bounds, gathered.reshape(rows, SIDE, SIDE))
     placed = placed.reshape(subbands, SIDE // 2, 2, SIDE)

time: 127 us -> 124 us (0.976)
  Pallas kernels: 126 us -> 123 us
    pallas_call x1, Pallas kernels: 6.32 us -> 3.84 us  [per_device(): pl.pallas_call(place_kernel, in_specs=[smem, far], out_specs=far, out_sha...]
where the time goes in v5:
time: 124 us; the launch traced here: 123 us
  Pallas kernels  123 us (99%)
    pallas_call x1, Pallas kernels, per_device(): pl.pallas_call(functools.partial(kernel, cosine_poly, sine_poly), out_sha...  119 us
    pallas_call x1, Pallas kernels, per_device(): pl.pallas_call(place_kernel, in_specs=[smem, far], out_specs=far, out_sha...  3.84 us

profile of v5, /device:TPU:1, one launch (start us, length us, event | category | flops | bytes accessed | tf_op | source)
XLA Modules:
  0.0 123.4 jit_solution(6359706256631995568)
XLA Ops:
  0.0 0.0 copy-start
  0.0 119.5 %beams.1 = bf16[2,64,128,128]{3,2,1,0:T(8,128)(2,1)S(1)} custom-call(f32[64]{0:T(128)} %delay_table.1, f32[32]{0:T(128)} %dm_table.1, s32[128]{0:T(128)} %dm_index.1, s32[2,128]{1,0:T(2,128)} %bitcast.10, f32[256]{0:T(256)} %constant.6.clone.cubes, s32[48,128]{1,0:T(8,128)} %bitcast.14, s32[2,128]{1,0:T(2,128)} %bitcast.11, bf16[2,96,8192]{2,1,0:T(8,128)(2,1)} %bitcast.13, ...), custom_call_target="tpu_custom_call" | custom-call | tf_op jit(solution)/shard_map/beams/pallas_call | solution.py:509
  119.5 0.0 copy-done
  119.5 3.8 %place.1 = bf16[256,128,128]{2,1,0:T(8,128)(2,1)} custom-call(s32[2,128]{1,0:T(2,128)S(1)} %bitcast.12, bf16[128,128,128]{2,1,0:T(8,128)(2,1)S(1)} %bitcast.9), custom_call_target="tpu_custom_call" | custom-call | tf_op jit(solution)/shard_map/place/pallas_call | solution.py:548
Async XLA Ops:
  0.0 119.5 %copy-start = (s32[128,2]{0,1:T(2,128)S(1)}, s32[128,2]{0,1:T(2,128)}, u32[]{:S(2)}) copy-start(s32[128,2]{0,1:T(2,128)} %param.14) | copy-start | bytes 3076
